TPU v7x, 32 devices: a whole 2x2x4 slice. The times are simulated.
32 devices in a mesh: band: 4 (over z), gy: 8 (over y, x, core).
Axes of the slice: x: 2, y: 2, z: 4, core: 2. Of those that a mesh axis runs over, the one named last changes fastest.
Arguments:
- orbitals: float32 [16, 32, 512, 256], P('band', None, 'gy'), may hold values from -11 to 11
- potentials: float32 [2, 32, 512, 256], P(None, None, 'gy'), may hold values from -1 to 3
- local_potential: float32 [32, 512, 256], P(None, 'gy'), may hold values from 0 to 1
- shifts: float32 [16], P('band'), may hold values from 0.05 to 0.8
Outputs:
- field_response: float32 [2, 32, 256, 512], P(None, 'band', 'gy')
All inputs are finite; a program needn't handle non-finite values.
Results may differ from a plain program's by a relative error of at most 0.0003.
Values sent between devices are 32-bit elements; how exact they have to be, the bound alone decides.
No kernel may reach another device: no remote copies, remote signals or barrier semaphores. Data moves between devices by JAX's collectives and lax.ppermute only.
A program may use at most 256 MiB of HBM per device.

v0:
```python
import jax
import jax.numpy as jnp
from jax import lax
from jax.sharding import PartitionSpec as P

NX = 256
NY = 512
NZ = 32
SWEEPS = 3


spread_half = 3.5
screening = 0.25


def extended(block, sides, width):
    for axis, dim in sides:
        count = lax.axis_size(axis)
        forward = [(i, i + 1) for i in range(count - 1)]
        backward = [(target, source) for source, target in forward]
        low = lax.ppermute(
            lax.slice_in_dim(block, block.shape[dim] - width, None, axis=dim), axis, forward
        )
        high = lax.ppermute(lax.slice_in_dim(block, 0, width, axis=dim), axis, backward)
        block = jnp.concatenate([low, block, high], axis=dim)
    return block


def sine_table(length):
    index = jnp.arange(1, length + 1, dtype=jnp.int32)
    phase = index[:, None] * index[None, :] % (2 * (length + 1))
    scale = jnp.sqrt(jnp.float32(2.0) / (length + 1))
    return scale * jnp.sin(jnp.float32(jnp.pi) * phase.astype(jnp.float32) / (length + 1))


def coulomb(z_index, x_index, y_index):
    wave_z = jnp.pi * (z_index.astype(jnp.float32) + 1.0) / (NZ + 1)
    wave_x = jnp.pi * (x_index.astype(jnp.float32) + 1.0) / (NX + 1)
    wave_y = jnp.pi * (y_index.astype(jnp.float32) + 1.0) / (NY + 1)
    total = (
        wave_z[:, None, None] * wave_z[:, None, None]
        + wave_x[None, :, None] * wave_x[None, :, None]
    )
    total = total + wave_y[None, None, :] * wave_y[None, None, :] + screening
    return jnp.sqrt(4.0 * jnp.pi / total)


def beside(field, axis):
    size = field.shape[axis]
    upper = lax.slice_in_dim(field, 1, size, axis=axis)
    lower = lax.slice_in_dim(field, 0, size - 1, axis=axis)
    pad_upper = tuple(((0, 1) if i == axis else (0, 0) for i in range(field.ndim)))
    pad_lower = tuple(((1, 0) if i == axis else (0, 0) for i in range(field.ndim)))
    return jnp.pad(upper, pad_upper) + jnp.pad(lower, pad_lower)


def operate(padded, local_potential, shift):
    center = padded[..., 1:-1, :]
    near = padded[..., 2:, :] + padded[..., :-2, :]
    near = near + beside(center, center.ndim - 1) + beside(center, center.ndim - 3)
    return (3.0 + local_potential + shift) * center - 0.5 * near


def chebyshev(source, apply_fn, shift):
    center_value = shift + spread_half
    ratio_start = center_value / spread_half
    weight_now = 1.0 / ratio_start
    direction = source / center_value
    residual = source
    iterate = jnp.zeros_like(source)
    for sweep in range(SWEEPS):
        iterate = iterate + direction
        residual = residual - apply_fn(direction)
        weight_next = 1.0 / (2.0 * ratio_start - weight_now)
        direction = (
            weight_next * weight_now * direction + 2.0 * weight_next / spread_half * residual
        )
        weight_now = weight_next
    return iterate + direction


def per_device(orbitals, potentials, local_potential, shifts):
    highest = lax.Precision.HIGHEST
    squares = orbitals * orbitals
    weighted = jnp.einsum("pzyx,bzyx->pb", potentials, squares, precision=highest)
    norms = jnp.sum(squares, axis=(1, 2, 3))
    weighted, norms = lax.psum((weighted, norms), "gy")
    coefficient = weighted / norms[None, :]
    shift = shifts[None, :, None, None, None]
    source = (potentials[:, None] - coefficient[:, :, None, None, None]) * orbitals[None]

    def apply_fn(field):
        padded = extended(field, (("gy", 3),), 1)
        return operate(padded, local_potential, shift)

    response = chebyshev(source, apply_fn, shift)
    density = -4.0 * jnp.sum(orbitals[None] * response, axis=1)
    z_share = NZ // lax.axis_size("band")
    table_z = sine_table(NZ)
    partial_value = jnp.einsum("kz,pzyx->pkyx", table_z, density, precision=highest)
    along_z = lax.psum_scatter(partial_value, "band", scatter_dimension=1, tiled=True)
    along_x = jnp.einsum("jx,pkyx->pkyj", sine_table(NX), along_z, precision=highest)
    x_share = NX // lax.axis_size("gy")
    z_index = lax.axis_index("band") * z_share + jnp.arange(z_share, dtype=jnp.int32)
    x_index = lax.axis_index("gy") * x_share + jnp.arange(x_share, dtype=jnp.int32)
    weight = coulomb(z_index, x_index, jnp.arange(NY, dtype=jnp.int32))
    table_y = sine_table(NY)
    return (
        jnp.einsum(
            "my,pkyj->pkjm",
            table_y,
            lax.all_to_all(along_x, "gy", split_axis=3, concat_axis=2, tiled=True),
            precision=highest,
        )
        * weight[None]
    )


def solution(mesh):
    placed = (
        P("band", None, "gy", None),
        P(None, None, "gy", None),
        P(None, "gy", None),
        P("band"),
    )
    return jax.shard_map(
        per_device,
        mesh=mesh,
        in_specs=placed,
        out_specs=P(None, "band", "gy", None),
        check_vma=False,
    )
```

profile of v0, /device:TPU:0, one launch (start us, length us, event | category | flops | bytes accessed | tf_op | source)
XLA Modules:
  0.0 577.3 jit_solution(10127989954610839993)
XLA Ops:
  6.5 4.9 multiply_reduce_fusion
  12.3 8.1 %copy.18 = f32[4,32,64,256]{3,1,2,0:T(8,128)} copy(f32[4,32,64,256]{3,2,1,0:T(8,128)S(1)} %copy-done.4) | data formatting | bytes 16777216 | tf_op args[0]
  20.4 4.4 copy.19
  24.8 93.1 %fusion.32 = f32[2,4]{1,0:T(2,128)S(1)} fusion(f32[2,32,64,256]{3,2,1,0:T(8,128)} %param.5, f32[4,32,64,256]{3,2,1,0:T(8,128)S(1)} %get-tuple-element.35), kind=kOutput, calls=%fused_computation.43 | convolution fusion | flops 50331648 | bytes 12582944 | tf_op jit(solution)/shard_map/pzyx,bzyx->pb/dot_general | solution.py:85
  118.4 15.1 %all-reduce.12 = (f32[2,4]{1,0:T(2,128)S(1)}, f32[4]{0:T(128)S(1)}) all-reduce(f32[2,4]{1,0:T(2,128)S(1)} %fusion.32, f32[4]{0:T(128)S(1)} %get-tuple-element.34), channel_id=1, replica_groups=mesh['band'=4,'gy'=8] {'gy'}, use_global_device_ids=true, to_apply=%region_0.0 | all-reduce | flops 12 | bytes 96 | tf_op jit(solution)/shard_map/psum | solution.py:87
  133.5 6.4 %fusion.22 = f32[2,4,32,64,256]{4,2,3,1,0:T(8,128)S(1)} fusion(f32[4]{0:T(128)S(1)} %get-tuple-element.40, f32[2,4]{1,0:T(2,128)S(1)} %broadcast_divide_fusion, f32[2,32,64,256]{3,1,2,0:T(8,128)} %copy.19, f32[4,32,64,256]{3,1,2,0:T(8,128)} %copy.18), kind=kLoop, calls=%fused_computation.31 | loop fusion | flops 12582912 | bytes 29360176 | tf_op jit(solution)/shard_map/div | solution.py:68
  141.3 3.5 collective-permute-start.1
  144.8 12.4 %fusion.109 = (f32[2,4,32,64,255]{4,2,3,1,0:T(8,128)}, f32[2,4,32,64,255]{4,2,3,1,0:T(8,128)}) fusion(f32[2,4,32,64,256]{4,2,3,1,0:T(8,128)S(1)} %fusion.22), kind=kLoop, calls=%fused_computation.133 | loop fusion | bytes 66846720 | tf_op jit(solution)/shard_map/slice | solution.py:50
  157.3 11.8 %fusion.110 = (f32[2,4,31,64,256]{4,2,3,1,0:T(8,128)}, f32[2,4,31,64,256]{4,2,3,1,0:T(8,128)}) fusion(f32[2,4,32,64,256]{4,2,3,1,0:T(8,128)S(1)} %fusion.22), kind=kLoop, calls=%fused_computation.134 | loop fusion | bytes 65011712 | tf_op jit(solution)/shard_map/slice | solution.py:50
  172.2 4.4 broadcast_add_fusion
  177.7 54.3 %multiply_add_fusion.1 = (f32[2,4,32,64,256]{4,2,3,1,0:T(8,128)}, f32[2,4,32,64,256]{4,2,3,1,0:T(8,128)}) fusion(f32[4]{0:T(128)S(1)} %get-tuple-element.37, f32[4]{0:T(128)S(1)} %get-tuple-element.38, f32[4]{0:T(128)S(1)} %get-tuple-element.40, f32[4,32,64,256]{3,1,2,0:T(8,128)} %copy.18, f32[2,4]{1,0:T(2,128)S(1)} %broadcast_divide_fusion, ...), kind=kLoop, calls=%fused_computation.29 | loop fusion | flops 71303168 | bytes 137756752 | tf_op jit(solution)/shard_map/add | solution.py:76
  232.0 25.6 %fusion.106 = (f32[2,4,32,64,255]{4,2,3,1,0:T(8,128)}, f32[2,4,32,64,255]{4,2,3,1,0:T(8,128)}) fusion(f32[2,4,32,64,256]{4,2,3,1,0:T(8,128)} %get-tuple-element.14), kind=kLoop, calls=%fused_computation.130 | loop fusion | bytes 66846720 | tf_op jit(solution)/shard_map/slice | solution.py:50
  262.2 12.1 %fusion.107 = (f32[2,4,31,64,256]{4,2,3,1,0:T(8,128)}, f32[2,4,31,64,256]{4,2,3,1,0:T(8,128)}) fusion(f32[2,4,32,64,256]{4,2,3,1,0:T(8,128)S(1)} %copy-done), kind=kLoop, calls=%fused_computation.131 | loop fusion | bytes 65011712 | tf_op jit(solution)/shard_map/slice | solution.py:50
  274.3 56.8 %multiply_add_fusion = (f32[2,4,32,64,256]{4,2,3,1,0:T(8,128)}, f32[2,4,32,64,256]{4,2,3,1,0:T(8,128)}) fusion(f32[2,4,32,64,256]{4,2,3,1,0:T(8,128)} %get-tuple-element.14, f32[4]{0:T(128)S(1)} %get-tuple-element.39, f32[4]{0:T(128)S(1)} %get-tuple-element.36, f32[2,4,32,64,256]{4,2,3,1,0:T(8,128)} %get-tuple-element.15, ...), kind=kLoop, calls=%fused_computation.28 | loop fusion | flops 58720256 | bytes 141951008 | tf_op jit(solution)/shard_map/add | solution.py:76
  331.1 25.6 %fusion.103 = (f32[2,4,32,64,255]{4,2,3,1,0:T(8,128)}, f32[2,4,32,64,255]{4,2,3,1,0:T(8,128)}) fusion(f32[2,4,32,64,256]{4,2,3,1,0:T(8,128)} %get-tuple-element.12), kind=kLoop, calls=%fused_computation.127 | loop fusion | bytes 66846720 | tf_op jit(solution)/shard_map/slice | solution.py:50
  358.0 3.8 collective-permute-start.5
  361.8 11.9 %fusion.104 = (f32[2,4,31,64,256]{4,2,3,1,0:T(8,128)}, f32[2,4,31,64,256]{4,2,3,1,0:T(8,128)}) fusion(f32[2,4,32,64,256]{4,2,3,1,0:T(8,128)S(1)} %copy-done.2), kind=kLoop, calls=%fused_computation.128 | loop fusion | bytes 65011712 | tf_op jit(solution)/shard_map/slice | solution.py:50
  373.8 58.8 %fusion.23 = f32[2,32,64,256]{3,1,2,0:T(8,128)} fusion(f32[2,4,32,64,256]{4,2,3,1,0:T(8,128)} %get-tuple-element.13, f32[2,4,31,64,256]{4,2,3,1,0:T(8,128)} %get-tuple-element.21, f32[2,4,31,64,256]{4,2,3,1,0:T(8,128)} %get-tuple-element.20, f32[2,4,32,64,255]{4,2,3,1,0:T(8,128)} %get-tuple-element.19, f32[2,4,32,64,255]{4,2,3,1,0:T(8,128)} %get-tuple-element.18, ...), kind=kLoop, calls=%fused_computation.32 | loop fusion | flops 91226112 | bytes 141951056 | tf_op jit(solution)/shard_map/reduce_sum | solution.py:97
  432.6 4.8 copy_multiply_fusion
  437.4 6.5 %fusion.29 = f32[2,32,64,256]{3,1,2,0:T(8,128)S(1)} fusion(f32[2,32,64,256]{3,2,1,0:T(8,128)S(1)} %copy_multiply_fusion, s32[32]{0:T(128)S(1)} %copy-done.6), kind=kOutput, calls=%fused_computation.40 | convolution fusion | flops 402663424 | bytes 8388736 | tf_op jit(solution)/shard_map/kz,pzyx->pkyx/dot_general | solution.py:100
  446.3 80.5 %reduce-scatter.5.cloned.1.call-done = f32[8,32768]{1,0:T(8,128)} async-done(((f32[32,32768]{1,0:T(8,128)}), f32[8,32768]{1,0:T(8,128)}) %reduce-scatter.5.cloned.1.call-update) | async-done | bytes 1048592
  534.1 3.7 all-to-all-start
  538.9 14.2 %all-to-all-done = f32[8,1,32768]{2,1,0:T(1,128)S(1)} async-done(((f32[8,1,32768]{2,1,0:T(1,128)}), f32[8,1,32768]{2,1,0:T(1,128)S(1)}, u32[]{:S(2)}, u32[]{:S(2)}) %all-to-all-start) | async-done | bytes 1048608 | tf_op jit(solution)/shard_map/all_to_all | solution.py:112
  562.1 7.9 %convolution_multiply_fusion = f32[2,8,32,512]{3,2,1,0:T(8,128)} fusion(f32[2,8,512,32]{2,3,1,0:T(8,128)S(1)} %all_to_all.16, f32[8,32,512]{2,1,0:T(8,128)} %divide_sqrt_fusion, s32[512]{0:T(512)S(1)} %iota_add_fusion), kind=kOutput, calls=%fused_computation.42 | convolution fusion | flops 1613496320 | bytes 2623488 | tf_op jit(solution)/shard_map/my,pkyj->pkjm/dot_general | solution.py:109
  (59 shorter events, 32.7 us)
Async XLA Ops:
  6.5 520.3 %reduce-scatter.5.cloned.1.call-start = ((), (), s32[]{:S(2)}) async-start(), calls=%async_computation.2 | async-start | bytes 5242880
  6.5 5.8 copy-start.4
  6.5 13.9 %copy-start.5 = (f32[2,32,64,256]{3,2,1,0:T(8,128)S(1)}, f32[2,32,64,256]{3,2,1,0:T(8,128)}, u32[]{:S(2)}) copy-start(f32[2,32,64,256]{3,2,1,0:T(8,128)} %param.5) | copy-start | bytes 12582916
  12.3 105.6 %copy-start.7 = (f32[4]{0:T(128)S(1)}, f32[4]{0:T(128)}, u32[]{:S(2)}) copy-start(f32[4]{0:T(128)} %param.7) | copy-start | bytes 52
  139.9 17.3 %copy-start.1 = (f32[2,4,32,64,256]{4,2,3,1,0:T(8,128)}, f32[2,4,32,64,256]{4,2,3,1,0:T(8,128)S(1)}, u32[]{:S(2)}) copy-start(f32[2,4,32,64,256]{4,2,3,1,0:T(8,128)S(1)} %fusion.22) | copy-start | bytes 50331652
  140.0 37.7 %collective-permute-start = (f32[2,4,32,1,256]{4,2,3,1,0:T(8,128)S(1)}, f32[2,4,32,1,256]{4,2,3,1,0:T(8,128)S(1)}, u32[]{:S(2)}, u32[]{:S(2)}) collective-permute-start(f32[2,4,32,1,256]{4,2,3,1,0:T(8,128)S(1)} %get-tuple-element.28), channel_id=1, source_target_pairs={{1,0},{2,1},{3,2},{4,3},{5,4},{6,5},{7,6},{9,8},{10,9},{11,10},{12... | collective-permute-start | bytes 786440 | tf_op jit(solution)/shard_map/ppermute | solution.py:24
  141.3 36.4 %collective-permute-start.1 = (f32[2,4,32,1,256]{4,2,3,1,0:T(8,128)S(1)}, f32[2,4,32,1,256]{4,2,3,1,0:T(8,128)S(1)}, u32[]{:S(2)}, u32[]{:S(2)}) collective-permute-start(f32[2,4,32,1,256]{4,2,3,1,0:T(8,128)S(1)} %get-tuple-element.29), channel_id=1, source_target_pairs={{0,1},{1,2},{2,3},{3,4},{4,5},{5,6},{6,7},{8,9},{9,10},{10,11},{11... | collective-permute-start | bytes 786440 | tf_op jit(solution)/shard_map/ppermute | solution.py:21
  169.1 8.6 %copy-start.3 = (f32[2,32,64,256]{3,1,2,0:T(8,128)S(1)}, f32[2,32,64,256]{3,1,2,0:T(8,128)}, u32[]{:S(2)}) copy-start(f32[2,32,64,256]{3,1,2,0:T(8,128)} %copy.19) | copy-start | bytes 12582916
  232.0 25.6 %copy-start = (f32[2,4,32,64,256]{4,2,3,1,0:T(8,128)S(1)}, f32[2,4,32,64,256]{4,2,3,1,0:T(8,128)}, u32[]{:S(2)}) copy-start(f32[2,4,32,64,256]{4,2,3,1,0:T(8,128)} %get-tuple-element.14) | copy-start | bytes 50331652
  257.6 16.6 %collective-permute-start.2 = (f32[2,4,32,1,256]{4,2,3,1,0:T(8,128)S(1)}, f32[2,4,32,1,256]{4,2,3,1,0:T(8,128)S(1)}, u32[]{:S(2)}, u32[]{:S(2)}) collective-permute-start(f32[2,4,32,1,256]{4,2,3,1,0:T(8,128)S(1)} %get-tuple-element.22), channel_id=1, source_target_pairs={{1,0},{2,1},{3,2},{4,3},{5,4},{6,5},{7,6},{9,8},{10,9},{11,10},{12... | collective-permute-start | bytes 786440 | tf_op jit(solution)/shard_map/ppermute | solution.py:24
  258.9 15.3 %collective-permute-start.3 = (f32[2,4,32,1,256]{4,2,3,1,0:T(8,128)S(1)}, f32[2,4,32,1,256]{4,2,3,1,0:T(8,128)S(1)}, u32[]{:S(2)}, u32[]{:S(2)}) collective-permute-start(f32[2,4,32,1,256]{4,2,3,1,0:T(8,128)S(1)} %get-tuple-element.23), channel_id=1, source_target_pairs={{0,1},{1,2},{2,3},{3,4},{4,5},{5,6},{6,7},{8,9},{9,10},{10,11},{11... | collective-permute-start | bytes 786440 | tf_op jit(solution)/shard_map/ppermute | solution.py:21
  331.1 25.6 %copy-start.2 = (f32[2,4,32,64,256]{4,2,3,1,0:T(8,128)S(1)}, f32[2,4,32,64,256]{4,2,3,1,0:T(8,128)}, u32[]{:S(2)}) copy-start(f32[2,4,32,64,256]{4,2,3,1,0:T(8,128)} %get-tuple-element.12) | copy-start | bytes 50331652
  356.7 17.1 %collective-permute-start.4 = (f32[2,4,32,1,256]{4,2,3,1,0:T(8,128)S(1)}, f32[2,4,32,1,256]{4,2,3,1,0:T(8,128)S(1)}, u32[]{:S(2)}, u32[]{:S(2)}) collective-permute-start(f32[2,4,32,1,256]{4,2,3,1,0:T(8,128)S(1)} %get-tuple-element.16), channel_id=1, source_target_pairs={{1,0},{2,1},{3,2},{4,3},{5,4},{6,5},{7,6},{9,8},{10,9},{11,10},{12... | collective-permute-start | bytes 786440 | tf_op jit(solution)/shard_map/ppermute | solution.py:24
  358.0 15.8 %copy-start.8 = (f32[4]{0:T(128)S(1)}, f32[4]{0:T(128)}, u32[]{:S(2)}) copy-start(f32[4]{0:T(128)} %get-tuple-element.7) | copy-start | bytes 52
  358.0 15.8 %copy-start.9 = (f32[4]{0:T(128)S(1)}, f32[4]{0:T(128)}, u32[]{:S(2)}) copy-start(f32[4]{0:T(128)} %broadcast_multiply_fusion) | copy-start | bytes 52
  358.0 15.7 %collective-permute-start.5 = (f32[2,4,32,1,256]{4,2,3,1,0:T(8,128)S(1)}, f32[2,4,32,1,256]{4,2,3,1,0:T(8,128)S(1)}, u32[]{:S(2)}, u32[]{:S(2)}) collective-permute-start(f32[2,4,32,1,256]{4,2,3,1,0:T(8,128)S(1)} %get-tuple-element.17), channel_id=1, source_target_pairs={{0,1},{1,2},{2,3},{3,4},{4,5},{5,6},{6,7},{8,9},{9,10},{10,11},{11... | collective-permute-start | bytes 786440 | tf_op jit(solution)/shard_map/ppermute | solution.py:21
  373.8 63.6 %copy-start.6 = (s32[32]{0:T(128)S(1)}, s32[32]{0:T(128)}, u32[]{:S(2)}) copy-start(s32[32]{0:T(128)} %iota_add_fusion.2) | copy-start | bytes 388
  534.1 19.1 %all-to-all-start = ((f32[8,1,32768]{2,1,0:T(1,128)}), f32[8,1,32768]{2,1,0:T(1,128)S(1)}, u32[]{:S(2)}, u32[]{:S(2)}) async-start(f32[8,1,32768]{2,1,0:T(1,128)} %reshape.130), calls=%async_computation | async-start | bytes 2097152 | tf_op jit(solution)/shard_map/all_to_all | solution.py:112
Sparse Core Ops, SparseCore 0:
  446.4 80.3 reduce-scatter.4
where the time goes:
time: 588 us; the launch traced here: 577 us
  other arithmetic  198 us (34%)
  local copies, waits for them, and re-layouts  128 us (22%)
  matrix products  110 us (19%)
  waiting for transfers between devices  94.7 us (16%)
  starting transfers between devices  18 us (3%)
  blocking collectives  15.1 us (3%)
  between operations  14.1 us (2%)
    add x2, other arithmetic, chebyshev(): weight_next * weight_now * direction  111 us
    slice x6, local copies, waits for them, and re-layouts, beside(): upper = lax.slice_in_dim(field, 1, size, axis=axis)  99.5 us
    dot_general x1, matrix products, per_device(): jnp.einsum('pzyx,bzyx->pb', potentials, squares, precision=highest)  93.1 us
    unnamed x2, waiting for transfers between devices  80.5 us
    reduce_sum x1, other arithmetic, per_device(): density = -4.0 * jnp.sum(orbitals[None] * response, axis=1)  58.8 us
    unnamed x26, local copies, waits for them, and re-layouts  20.2 us
    psum x1, blocking collectives, per_device(): weighted, norms = lax.psum((weighted, norms), 'gy')  15.1 us
    all_to_all x1, waiting for transfers between devices, per_device(): lax.all_to_all(along_x, 'gy', split_axis=3, concat_axis=2, tiled=True)  14.2 us
  transfers between devices with their start and end apart: 8, of which 2 were waited for; matrix products, arithmetic and copies ran while one was open for 10% of the time, Pallas kernels for 0%

commit v1 on v0

v1 whole, which is shorter than its diff:
```python
import functools

import jax
import jax.numpy as jnp
import numpy as np
from jax import lax
from jax.experimental import pallas as pl
from jax.experimental.pallas import tpu as pltpu
from jax.sharding import PartitionSpec as P

SWEEPS = 3
HALO = SWEEPS
TILE = 8
LANES = 128

spread_half = 3.5
screening = 0.25


def sine_values(length):
    index = np.arange(1, length + 1)
    phase = index[:, None] * index[None, :] % (2 * (length + 1))
    return np.sqrt(2.0 / (length + 1)) * np.sin(np.pi * phase / (length + 1))


def two_parts(values):
    whole = np.asarray(values, np.float32)
    high = whole.astype(jnp.bfloat16)
    low = (whole - high.astype(np.float32)).astype(jnp.bfloat16)
    return np.stack([high, low])


def split(value):
    high = value.astype(jnp.bfloat16)
    low = (value - high.astype(jnp.float32)).astype(jnp.bfloat16)
    return high, low


def product(a, b, contract):
    dims = (contract, ((), ()))
    dot = functools.partial(lax.dot_general, dimension_numbers=dims, preferred_element_type=jnp.float32)
    return dot(a[0], b[0]) + dot(a[1], b[0]) + dot(a[0], b[1])


def coulomb(z_index, x_index, y_index, sizes):
    nz, nx, ny = sizes
    wave_z = jnp.pi * (z_index.astype(jnp.float32) + 1.0) / (nz + 1)
    wave_x = jnp.pi * (x_index.astype(jnp.float32) + 1.0) / (nx + 1)
    wave_y = jnp.pi * (y_index.astype(jnp.float32) + 1.0) / (ny + 1)
    total = (
        wave_z[:, None, None] * wave_z[:, None, None]
        + wave_x[None, :, None] * wave_x[None, :, None]
    )
    total = total + wave_y[None, None, :] * wave_y[None, None, :] + screening
    return jnp.sqrt(4.0 * jnp.pi / total)


def project_kernel(orbitals, potentials, out):
    count, planes, rows, width = orbitals.shape
    npot = potentials.shape[0]
    halves = width // LANES

    @pl.when(pl.program_id(0) == 0)
    def _():
        out[...] = jnp.zeros_like(out)

    def fold(value):
        return jnp.sum(value.reshape(rows // TILE, TILE, LANES), axis=0)

    def body(z, _):
        for half in range(halves):
            lanes = slice(half * LANES, (half + 1) * LANES)
            potential = [potentials[p, z, :, lanes] for p in range(npot)]
            for n in range(count):
                value = orbitals[n, z, :, lanes]
                square = value * value
                for p in range(npot):
                    out[p * count + n] += fold(potential[p] * square)
                out[npot * count + n] += fold(square)
        return 0

    lax.fori_loop(0, planes, body, 0)


def project(orbitals, potentials):
    count, planes, rows, width = orbitals.shape
    npot = potentials.shape[0]
    step = 4
    sums = (npot + 1) * count
    partial_sums = pl.pallas_call(
        project_kernel,
        grid=(planes // step,),
        in_specs=[
            pl.BlockSpec((count, step, rows, width), lambda i: (0, i, 0, 0)),
            pl.BlockSpec((npot, step, rows, width), lambda i: (0, i, 0, 0)),
        ],
        out_specs=pl.BlockSpec((sums, TILE, LANES), lambda i: (0, 0, 0)),
        out_shape=jax.ShapeDtypeStruct((sums, TILE, LANES), jnp.float32),
        compiler_params=pltpu.CompilerParams(vmem_limit_bytes=40 << 20),
    )(orbitals, potentials)
    return jnp.sum(partial_sums, axis=1)


def stencil_kernel(
    geometry,
    sums, constants, edges, z_table, x_table, neighbours,
    orbitals, potentials, local, low, high,
    mine, partner, far,
    orb, pot, loc, src, one, two, density, spectrum, sems,
):
    first_p, npot, all_pots, count, start, rows, strip, group = geometry
    planes = local.shape[0]
    width = local.shape[2]
    halves = width // LANES
    padded = rows + 2 * TILE
    f32 = jnp.float32

    begin, end = max(start - TILE, 0), min(start + rows + TILE, strip)
    place = begin - (start - TILE)
    copies = {}
    slot = 0
    fields = [("loc", 0, local, None, loc, all_pots + count)]
    for p in range(npot):
        fields.append(("pot", p, potentials, first_p + p, pot, count + first_p + p))
    for n in range(count):
        fields.append(("orb", n, orbitals, n, orb, n))
    for name, position, source, index, target, halo_index in fields:
        started = []
        for half in range(halves):
            lanes = pl.ds(half * LANES, LANES)
            whole = source if index is None else source.at[index]
            into = target.at[half] if index is None else target.at[half, position]
            pieces = [(whole.at[:, pl.ds(begin, end - begin), lanes], into.at[:, pl.ds(place, end - begin), :])]
            if start - TILE < 0:
                pieces.append((low.at[halo_index, :, :, lanes], into.at[:, pl.ds(0, TILE), :]))
            if start + rows + TILE > strip:
                pieces.append((high.at[halo_index, :, :, lanes], into.at[:, pl.ds(padded - TILE, TILE), :]))
            for a, b in pieces:
                copy = pltpu.make_async_copy(a, b, sems.at[slot])
                copy.start()
                started.append(copy)
                slot += 1
        copies[name, position] = started

    def wait(name, position):
        for copy in copies[name, position]:
            copy.wait()

    for field in (src, one, two):
        for half in range(halves):
            for z in (0, planes + 1):
                field[half, z] = jnp.zeros(field.shape[2:], f32)

    totals = jnp.sum(sums[...], axis=1, keepdims=True)
    first_edge, last_edge = edges[0] == 1, edges[1] == 1
    if start > 0:
        first_edge = None
    if start + rows < strip:
        last_edge = None
    band_matrix = neighbours[...]

    wait("loc", 0)

    def weights(z, _):
        for half in range(halves):
            loc[half, z] = 1.0 - 2.0 * loc[half, z]
        return 0

    lax.fori_loop(0, planes, weights, 0)

    def apply(field, offset, size, loc_offset, finish):
        def body(step, _):
            z0 = step * group
            centers = []
            for i in range(group):
                centers.append([field[h, z0 + i + 1, pl.ds(offset, size), :] for h in range(halves)])
            joined = jnp.concatenate([jnp.concatenate(c, axis=-1) for c in centers], axis=0)
            upper, lower = split(joined)
            near = jnp.dot(upper, band_matrix, preferred_element_type=f32)
            near = near + jnp.dot(lower, band_matrix, preferred_element_type=f32)
            for i in range(group):
                z = z0 + i
                for h in range(halves):
                    total = near[i * size:(i + 1) * size, h * LANES:(h + 1) * LANES]
                    total = total + (field[h, z + 1, pl.ds(offset - 1, size), :] + field[h, z + 1, pl.ds(offset + 1, size), :])
                    total = total + (field[h, z, pl.ds(offset, size), :] + field[h, z + 2, pl.ds(offset, size), :])
                    finish(z, h, total, centers[i][h], loc[h, z, pl.ds(loc_offset, size), :])
            return 0

        lax.fori_loop(0, planes // group, body, 0)

    def clear(field, where, row, size):
        if where is not None:
            @pl.when(where)
            def _():
                for h in range(halves):
                    field[h, :, pl.ds(row, size), :] = jnp.zeros((planes + 2, size, LANES), f32)

    for n in range(count):
        wait("orb", n)
        square, linear, constant, scale = (constants[n, i] for i in range(4))
        for p in range(npot):
            if n == 0:
                wait("pot", p)
            pair = (first_p + p) * count + n
            norm = all_pots * count + n
            coefficient = totals[pair:pair + 1] / totals[norm:norm + 1]

            def source(z, _):
                for h in range(halves):
                    src[h, z + 1] = (pot[h, p, z] - coefficient) * orb[h, n, z]
                return 0

            lax.fori_loop(0, planes, source, 0)

            def finish_one(z, h, near, center, weight):
                one[h, z + 1, pl.ds(0, rows + TILE), :] = near + (weight + square) * center

            apply(src, TILE - 2, rows + TILE, TILE - 2, finish_one)
            clear(one, first_edge, 0, 2)
            clear(one, last_edge, rows + 2, 2)

            def finish_two(z, h, near, center, weight):
                two[h, z + 1] = near + weight * center + linear * src[h, z + 1, pl.ds(TILE - 1, rows + TILE), :]

            apply(one, 1, rows + TILE, TILE - 1, finish_two)
            clear(two, first_edge, 0, 1)
            clear(two, last_edge, rows + 1, 1)

            def finish_three(z, h, near, center, weight):
                value = near + weight * center + constant * src[h, z + 1, pl.ds(TILE, rows), :]
                value = value * (orb[h, n, z, pl.ds(TILE, rows), :] * scale)
                if n > 0:
                    value = value + density[h, p, z]
                density[h, p, z] = value

            apply(two, 1, rows, TILE, finish_three)

    z_parts = (z_table[0], z_table[1])
    x_parts = (x_table[0], x_table[1])
    share = mine.shape[2]
    block = min(share, 2 * LANES)
    for p in range(npot):
        for tile in range(rows // TILE):
            span = pl.ds(tile * TILE, TILE)
            value = jnp.concatenate(
                [density[h, p, :, span, :].reshape(planes * TILE, LANES) for h in range(halves)], axis=-1
            )
            value = product(z_parts, split(value), ((1,), (0,)))
            spectrum[:, span, :] = value.reshape(planes, TILE, width)
        for piece in range(planes * rows // block):
            at = piece * block
            value = spectrum[at // rows:(at + block) // rows].reshape(block, width)
            value = product(x_parts, split(value), ((1,), (1,)))
            if at < share:
                mine[p, :, at:at + block] = value
            elif at < 2 * share:
                partner[p, :, at - share:at - share + block] = value
            else:
                far[p, :, at - 2 * share:at - 2 * share + block] = value


def stencil(first_p, npot, start, rows, group, sums, constants, edges, tables, fields, halos):
    orbitals, potentials, local = fields
    count, planes, strip, width = orbitals.shape
    all_pots = potentials.shape[0]
    halves = width // LANES
    padded = rows + 2 * TILE
    share = planes * rows // 4
    geometry = (first_p, npot, all_pots, count, start, rows, strip, group)
    vmem = pl.BlockSpec(memory_space=pltpu.VMEM)
    smem = pl.BlockSpec(memory_space=pltpu.SMEM)
    anywhere = pl.BlockSpec(memory_space=pl.ANY)
    f32 = jnp.float32
    return pl.pallas_call(
        functools.partial(stencil_kernel, geometry),
        in_specs=[vmem, smem, smem, vmem, vmem, vmem] + [anywhere] * 5,
        out_specs=[vmem] * 3,
        out_shape=[
            jax.ShapeDtypeStruct((npot, width, share), f32),
            jax.ShapeDtypeStruct((npot, width, share), f32),
            jax.ShapeDtypeStruct((npot, width, 2 * share), f32),
        ],
        scratch_shapes=[
            pltpu.VMEM((halves, count, planes, padded, LANES), f32),
            pltpu.VMEM((halves, npot, planes, padded, LANES), f32),
            pltpu.VMEM((halves, planes, padded, LANES), f32),
            pltpu.VMEM((halves, planes + 2, padded, LANES), f32),
            pltpu.VMEM((halves, planes + 2, padded, LANES), f32),
            pltpu.VMEM((halves, planes + 2, rows + TILE, LANES), f32),
            pltpu.VMEM((halves, npot, planes, rows, LANES), f32),
            pltpu.VMEM((planes, rows, width), f32),
            pltpu.SemaphoreType.DMA(((1 + npot + count) * halves * 3,)),
        ],
        compiler_params=pltpu.CompilerParams(vmem_limit_bytes=56 << 20),
    )(sums, constants, edges, *tables, orbitals, potentials, local, *halos)


def finish_kernel(received, table, weight, out):
    parts, x_share, lanes = received.shape
    z_share = out.shape[0]
    strip = lanes // z_share
    table_parts = (table[0], table[1])
    lane = lax.broadcasted_iota(jnp.int32, (x_share, LANES), 1)
    lower = lane < strip
    for pair in range(z_share // 2):
        columns = slice(pair * LANES, (pair + 1) * LANES)
        blocks = [received[i, :, columns] for i in range(parts)]
        rolled = [pltpu.roll(b, strip, 1) for b in blocks]
        even = [jnp.where(lower, blocks[i], rolled[i + 1]) for i in range(0, parts, 2)]
        odd = [jnp.where(lower, rolled[i], blocks[i + 1]) for i in range(0, parts, 2)]
        both = jnp.concatenate([jnp.concatenate(even, axis=-1), jnp.concatenate(odd, axis=-1)], axis=0)
        value = product(split(both), table_parts, ((1,), (0,)))
        out[2 * pair] = value[:x_share] * weight[2 * pair]
        out[2 * pair + 1] = value[x_share:] * weight[2 * pair + 1]


def finish(received, table, weight):
    vmem = pl.BlockSpec(memory_space=pltpu.VMEM)
    return pl.pallas_call(
        finish_kernel,
        in_specs=[vmem] * 3,
        out_specs=vmem,
        out_shape=jax.ShapeDtypeStruct(weight.shape, jnp.float32),
        compiler_params=pltpu.CompilerParams(vmem_limit_bytes=40 << 20),
    )(received, table, weight)


def total_over(values, axis):
    count = lax.axis_size(axis)
    step = 1
    while step < count:
        values = values + lax.ppermute(values, axis, [(i, i ^ step) for i in range(count)])
        step *= 2
    return values


def per_device(orbitals, potentials, local_potential, shifts):
    f32 = jnp.float32
    count, nz, strip, nx = orbitals.shape
    npot = potentials.shape[0]
    gy, bands = lax.axis_size("gy"), lax.axis_size("band")
    ny = strip * gy
    band, place = lax.axis_index("band"), lax.axis_index("gy")
    z_share, x_share = nz // bands, nx // gy

    def edge(rows):
        cut = [lax.slice_in_dim(f, *rows, axis=f.ndim - 2) for f in (orbitals, potentials, local_potential[None])]
        return jnp.concatenate(cut, axis=0)

    forward = [(i, i + 1) for i in range(gy - 1)]
    backward = [(b, a) for a, b in forward]
    low = lax.ppermute(edge((strip - HALO, strip)), "gy", forward)
    high = lax.ppermute(edge((0, HALO)), "gy", backward)
    low = jnp.pad(low, ((0, 0), (0, 0), (TILE - HALO, 0), (0, 0)))
    high = jnp.pad(high, ((0, 0), (0, 0), (0, TILE - HALO), (0, 0)))

    sums = total_over(project(orbitals, potentials), "gy")

    excess = shifts / spread_half
    s = 1.0 + excess
    less_one = excess * (2.0 + excess)
    fourth = 1.0 + 8.0 * s * s * less_one
    unit = 2.0 * spread_half
    constants = jnp.stack(
        [
            unit * s,
            unit * unit * less_one,
            unit**3 * s * less_one,
            -32.0 / (spread_half * unit**3) / fourth,
        ],
        axis=1,
    )
    edges = jnp.stack([place == 0, place == gy - 1]).astype(jnp.int32)

    sine_z = sine_values(nz)
    paired = bands == 4
    if paired:
        orders = [[b, b ^ 1] + ([2, 3] if b < 2 else [1, 0]) for b in range(bands)]
    else:
        orders = [list(range(bands))] * bands
    by_band = []
    for order in orders:
        index = np.concatenate([np.arange(z_share) + z_share * o for o in order])
        by_band.append(two_parts(np.kron(sine_z[index], np.eye(TILE))))
    z_table = lax.dynamic_index_in_dim(jnp.asarray(np.stack(by_band)), band, 0, keepdims=False)
    near = np.eye(nx, k=1) + np.eye(nx, k=-1)
    tables = (z_table, jnp.asarray(two_parts(sine_values(nx))), jnp.asarray(near, jnp.bfloat16))
    y_table = jnp.asarray(two_parts(sine_values(ny)))

    z_index = band * z_share + jnp.arange(z_share, dtype=jnp.int32)
    x_index = place * x_share + jnp.arange(x_share, dtype=jnp.int32)
    weight = coulomb(z_index, x_index, jnp.arange(ny, dtype=jnp.int32), (nz, nx, ny))

    outs = []
    for p in range(npot):
        mine, partner, far = stencil(
            p, 1, 0, strip, 4, sums, constants, edges, tables,
            (orbitals, potentials, local_potential), (low, high),
        )
        share = mine.shape[2]
        if paired:
            far = far + lax.ppermute(far, "band", [(0, 1), (3, 2)])
            back = lax.ppermute(far, "band", [(1, 2), (2, 1)])
            mine = mine + back[..., :share]
            partner = partner + back[..., share:]
            total = mine + lax.ppermute(partner, "band", [(0, 1), (1, 0), (2, 3), (3, 2)])
        else:
            joined = jnp.concatenate([mine, partner, far], axis=2)
            total = lax.psum_scatter(joined, "band", scatter_dimension=2, tiled=True)
        spread = total.reshape(gy, x_share, -1)
        received = lax.all_to_all(spread, "gy", split_axis=0, concat_axis=0, tiled=True)
        if paired:
            outs.append(finish(received, y_table, weight))
        else:
            terms = received.reshape(gy, x_share, z_share, strip)
            table = jnp.asarray(sine_values(ny), f32).reshape(gy, strip, ny)
            value = jnp.einsum("sjky,sym->kjm", terms, table, precision=lax.Precision.HIGHEST)
            outs.append(value * weight)
    return jnp.stack(outs)


def solution(mesh):
    placed = (
        P("band", None, "gy", None),
        P(None, None, "gy", None),
        P(None, "gy", None),
        P("band"),
    )
    return jax.shard_map(
        per_device,
        mesh=mesh,
        in_specs=placed,
        out_specs=P(None, "band", "gy", None),
        check_vma=False,
    )
```

time: 588 us -> 190 us (0.32); the launches traced: 577 us -> 190 us
  other arithmetic: 198 us -> 9.96 us
  local copies, waits for them, and re-layouts: 128 us -> 11.1 us
  matrix products: 110 us -> 0 us
  Pallas kernels: 0 us -> 77.7 us
  waiting for transfers between devices: 94.7 us -> 43.5 us
  starting transfers between devices: 18 us -> 47.2 us
  blocking collectives: 15.1 us -> 0 us
  between operations: 14.1 us -> 0.34 us
    add x7 -> x9, other arithmetic: 118 us -> 7.2 us  [the longest x2 4.29 us: per_device(): mine + lax.ppermute(partner, 'band', [(0, 1), (1, 0), (2, 3), (3, 2)])]
    dot_general x4 -> x0, matrix products: 110 us -> none  [the longest x1 93.1 us: per_device(): jnp.einsum('pzyx,bzyx->pb', potentials, squares, precision=highest)]
    slice x9 -> x3, local copies, waits for them, and re-layouts: 99.6 us -> 1.99 us  [edge(): lax.slice_in_dim(f, *rows, axis=f.ndim - 2)]
    unnamed x2 -> x0, waiting for transfers between devices: 80.5 us -> none
    pallas_call x0 -> x5, Pallas kernels: none -> 77.7 us  [the longest x2 72.3 us: stencil(): pl.pallas_call(functools.partial(stencil_kernel, geometry), in_specs=[vme...]
    reduce_sum x2 -> x1, other arithmetic: 63.7 us -> 0.02 us  [project(): return jnp.sum(partial_sums, axis=1)]
    ppermute x6 -> x11, waiting for transfers between devices: 0.02 us -> 30.3 us  [the longest x2 17.2 us: per_device(): far = far + lax.ppermute(far, 'band', [(0, 1), (3, 2)])]
    ppermute x6 -> x11, starting transfers between devices: 14.4 us -> 40.2 us  [the longest x2 24.5 us: per_device(): lax.ppermute(partner, 'band', [(0, 1), (1, 0), (2, 3), (3, 2)])]
  transfers between devices with their start and end apart: 8 -> 13, of which waited for: 2 -> 6; matrix products, arithmetic and copies ran while one was open for 10% -> 7% of each run, Pallas kernels for 0% -> 22%
where the time goes in v1:
time: 190 us
  Pallas kernels  77.7 us (41%)
  starting transfers between devices  47.2 us (25%)
  waiting for transfers between devices  43.5 us (23%)
  local copies, waits for them, and re-layouts  11.1 us (6%)
  other arithmetic  9.96 us (5%)
    pallas_call x2, Pallas kernels, stencil(): pl.pallas_call(functools.partial(stencil_kernel, geometry), in_specs=[vme...  72.3 us
    ppermute x2, starting transfers between devices, per_device(): lax.ppermute(partner, 'band', [(0, 1), (1, 0), (2, 3), (3, 2)])  24.5 us
    ppermute x2, waiting for transfers between devices, per_device(): far = far + lax.ppermute(far, 'band', [(0, 1), (3, 2)])  17.2 us
    all_to_all x2, waiting for transfers between devices, per_device(): lax.all_to_all(spread, 'gy', split_axis=0, concat_axis=0, tiled=True)  13.3 us
    ppermute x3, waiting for transfers between devices, total_over(): lax.ppermute(values, axis, [(i, i ^ step) for i in range(count)])  10.8 us
    all_to_all x2, starting transfers between devices, per_device(): lax.all_to_all(spread, 'gy', split_axis=0, concat_axis=0, tiled=True)  6.99 us
    ppermute x2, starting transfers between devices, per_device(): far = far + lax.ppermute(far, 'band', [(0, 1), (3, 2)])  5.17 us
    ppermute x3, starting transfers between devices, total_over(): lax.ppermute(values, axis, [(i, i ^ step) for i in range(count)])  4.96 us
  transfers between devices with their start and end apart: 13, of which 6 were waited for; matrix products, arithmetic and copies ran while one was open for 7% of the time, Pallas kernels for 22%

profile of v1, /device:TPU:0, one launch (start us, length us, event | category | flops | bytes accessed | tf_op | source)
XLA Modules:
  0.0 189.8 jit_solution(11064940531084780907)
XLA Ops:
  0.0 3.0 %copy.29 = f32[32,64,256]{2,0,1:T(8,128)S(1)} copy(f32[32,64,256]{2,1,0:T(8,128)} %local.3) | data formatting | bytes 4194304 | tf_op args[2]
  3.0 1.9 fusion.3
  5.2 2.7 %collective-permute-start.3 = (f32[7,32,3,256]{3,1,2,0:T(8,128)S(1)}, f32[7,32,3,256]{3,1,2,0:T(8,128)S(1)}, u32[]{:S(2)}, u32[]{:S(2)}) collective-permute-start(f32[7,32,3,256]{3,1,2,0:T(8,128)S(1)} %pad_maximum_fusion.1), channel_id=1, source_target_pairs={{0,1},{1,2},{2,3},{3,4},{4,5},{5,6},{6,7},{8,9},{9,10},{10,11},{11... | collective-permute-start | bytes 2064392 | tf_op jit(solution)/shard_map/ppermute | solution.py:353
  9.4 2.9 %shard_map.82 = f32[12,8,128]{2,1,0:T(8,128)S(1)} custom-call(f32[4,32,64,256]{3,2,1,0:T(8,128)S(1)} %copy-done, f32[2,32,64,256]{3,2,1,0:T(8,128)S(1)} %copy-done.1), custom_call_target="tpu_custom_call" | custom-call | tf_op jit(solution)/shard_map/pallas_call | solution.py:90
  12.3 3.3 %collective-permute-start = (f32[12,128]{1,0:T(8,128)S(1)}, f32[12,128]{1,0:T(8,128)S(1)}, u32[]{:S(2)}, u32[]{:S(2)}) collective-permute-start(f32[12,128]{1,0:T(8,128)S(1)} %reduce_sum.9), channel_id=1, source_target_pairs={{0,1},{1,0},{2,3},{3,2},{4,5},{5,4},{6,7},{7,6},{8,9},{9,8},{10,11... | collective-permute-start | bytes 18440 | tf_op jit(solution)/shard_map/ppermute | solution.py:333
  15.5 1.7 dynamic-slice_bitcast_fusion.z_table
  17.6 1.7 collective-permute-start.1
  20.0 7.7 %collective-permute-done.1 = f32[12,128]{1,0:T(8,128)S(1)} collective-permute-done((f32[12,128]{1,0:T(8,128)S(1)}, f32[12,128]{1,0:T(8,128)S(1)}, u32[]{:S(2)}, u32[]{:S(2)}) %collective-permute-start.1) | collective-permute-done | bytes 6176 | tf_op jit(solution)/shard_map/ppermute | solution.py:333
  28.2 3.1 %collective-permute-done.2 = f32[12,128]{1,0:T(8,128)S(1)} collective-permute-done((f32[12,128]{1,0:T(8,128)S(1)}, f32[12,128]{1,0:T(8,128)S(1)}, u32[]{:S(2)}, u32[]{:S(2)}) %collective-permute-start.2) | collective-permute-done | bytes 6176 | tf_op jit(solution)/shard_map/ppermute | solution.py:333
  32.4 1.5 pad.8.low
  35.7 34.0 %shard_map.83 = (f32[1,256,512]{2,1,0:T(8,128)}, f32[1,256,512]{2,1,0:T(8,128)}, f32[1,256,1024]{2,1,0:T(8,128)}) custom-call(f32[12,128]{1,0:T(8,128)} %add.136.sums, f32[4,4]{1,0:T(4,128)} %pad_maximum_fusion.3.constants, s32[2]{0:T(128)} %add_convert_fusion.edges, bf16[2,256,256]{2,1,0:T(8,128)(2,1)} %dynamic-slice_bitcast_fusion.z_table, ...), custom_call_target="tpu_custom_call" | custom-call | tf_op jit(solution)/shard_map/pallas_call | solution.py:275
  69.7 3.7 %collective-permute-start.5 = (f32[1,256,1024]{2,1,0:T(8,128)}, f32[1,256,1024]{2,1,0:T(8,128)S(1)}, u32[]{:S(2)}, u32[]{:S(2)}) collective-permute-start(f32[1,256,1024]{2,1,0:T(8,128)} %get-tuple-element.12), channel_id=1, source_target_pairs={{0,8},{24,16},{1,9},{25,17},{2,10},{26,18},{3,11},{27,19},{4,12},{... | collective-permute-start | bytes 3145736 | tf_op jit(solution)/shard_map/ppermute | solution.py:403
  73.4 38.4 %shard_map.85 = (f32[1,256,512]{2,1,0:T(8,128)}, f32[1,256,512]{2,1,0:T(8,128)}, f32[1,256,1024]{2,1,0:T(8,128)}) custom-call(f32[12,128]{1,0:T(8,128)} %add.136.sums, f32[4,4]{1,0:T(4,128)} %pad_maximum_fusion.3.constants, s32[2]{0:T(128)} %add_convert_fusion.edges, bf16[2,256,256]{2,1,0:T(8,128)(2,1)} %dynamic-slice_bitcast_fusion.z_table, ...), custom_call_target="tpu_custom_call" | custom-call | tf_op jit(solution)/shard_map/pallas_call | solution.py:275
  111.8 1.5 collective-permute-start.8
  114.4 17.2 %collective-permute-done.8 = f32[1,256,1024]{2,1,0:T(8,128)S(1)} collective-permute-done((f32[1,256,1024]{2,1,0:T(8,128)}, f32[1,256,1024]{2,1,0:T(8,128)S(1)}, u32[]{:S(2)}, u32[]{:S(2)}) %collective-permute-start.8) | collective-permute-done | bytes 1048608 | tf_op jit(solution)/shard_map/ppermute | solution.py:403
  133.3 5.1 %collective-permute-start.7 = (f32[1,256,512]{2,1,0:T(8,128)}, f32[1,256,512]{2,1,0:T(8,128)}, u32[]{:S(2)}, u32[]{:S(2)}) collective-permute-start(f32[1,256,512]{2,1,0:T(8,128)} %slice_add_fusion.2), channel_id=1, source_target_pairs={{0,8},{8,0},{16,24},{24,16},{1,9},{9,1},{17,25},{25,17},{2,10},{10... | collective-permute-start | bytes 1572872 | tf_op jit(solution)/shard_map/ppermute | solution.py:407
  139.6 19.4 %collective-permute-start.10 = (f32[1,256,512]{2,1,0:T(8,128)S(1)}, f32[1,256,512]{2,1,0:T(8,128)}, u32[]{:S(2)}, u32[]{:S(2)}) collective-permute-start(f32[1,256,512]{2,1,0:T(8,128)S(1)} %slice_add_fusion), channel_id=1, source_target_pairs={{0,8},{8,0},{16,24},{24,16},{1,9},{9,1},{17,25},{25,17},{2,10},{10... | collective-permute-start | bytes 1572872 | tf_op jit(solution)/shard_map/ppermute | solution.py:407
  159.0 2.2 %fusion.1 = f32[1,256,512]{2,1,0:T(8,128)} fusion(f32[1,256,512]{2,1,0:T(8,128)} %collective-permute-done.7, f32[1,256,512]{2,1,0:T(8,128)} %get-tuple-element.11, f32[1,256,1024]{2,1,0:T(8,128)S(1)} %collective-permute-done.6), kind=kLoop, calls=%fused_computation.9 | loop fusion | flops 262144 | bytes 2097152 | tf_op jit(solution)/shard_map/add | solution.py:407
  161.1 3.5 %all-to-all-start = ((f32[8,32,512]{2,1,0:T(8,128)}), f32[8,32,512]{2,1,0:T(8,128)S(1)}, u32[]{:S(2)}, u32[]{:S(2)}) async-start(f32[8,32,512]{2,1,0:T(8,128)} %bitcast.8), calls=%async_computation | async-start | bytes 1048576 | tf_op jit(solution)/shard_map/all_to_all | solution.py:412
  164.7 2.3 %collective-permute-done.10 = f32[1,256,512]{2,1,0:T(8,128)} collective-permute-done((f32[1,256,512]{2,1,0:T(8,128)S(1)}, f32[1,256,512]{2,1,0:T(8,128)}, u32[]{:S(2)}, u32[]{:S(2)}) %collective-permute-start.10) | collective-permute-done | bytes 524320 | tf_op jit(solution)/shard_map/ppermute | solution.py:407
  167.0 2.1 %fusion = f32[1,256,512]{2,1,0:T(8,128)} fusion(f32[1,256,512]{2,1,0:T(8,128)} %collective-permute-done.10, f32[1,256,512]{2,1,0:T(8,128)} %get-tuple-element.14, f32[1,256,1024]{2,1,0:T(8,128)S(1)} %collective-permute-done.9), kind=kLoop, calls=%fused_computation.6 | loop fusion | flops 262144 | bytes 2097152 | tf_op jit(solution)/shard_map/add | solution.py:407
  169.1 5.2 %all-to-all-done.received = f32[8,32,512]{2,1,0:T(8,128)S(1)} async-done(((f32[8,32,512]{2,1,0:T(8,128)}), f32[8,32,512]{2,1,0:T(8,128)S(1)}, u32[]{:S(2)}, u32[]{:S(2)}) %all-to-all-start) | async-done | bytes 524320 | tf_op jit(solution)/shard_map/all_to_all | solution.py:412
  174.3 3.5 %all-to-all-start.1 = ((f32[8,32,512]{2,1,0:T(8,128)}), f32[8,32,512]{2,1,0:T(8,128)S(1)}, u32[]{:S(2)}, u32[]{:S(2)}) async-start(f32[8,32,512]{2,1,0:T(8,128)} %bitcast.10), calls=%async_computation.1 | async-start | bytes 1048576 | tf_op jit(solution)/shard_map/all_to_all | solution.py:412
  179.4 8.1 %all-to-all-done.1.received = f32[8,32,512]{2,1,0:T(8,128)S(1)} async-done(((f32[8,32,512]{2,1,0:T(8,128)}), f32[8,32,512]{2,1,0:T(8,128)S(1)}, u32[]{:S(2)}, u32[]{:S(2)}) %all-to-all-start.1) | async-done | bytes 524320 | tf_op jit(solution)/shard_map/all_to_all | solution.py:412
  (59 shorter events, 14.2 us)
Async XLA Ops:
  0.0 5.0 %copy-start.1 = (f32[2,32,64,256]{3,2,1,0:T(8,128)S(1)}, f32[2,32,64,256]{3,2,1,0:T(8,128)}, u32[]{:S(2)}) copy-start(f32[2,32,64,256]{3,2,1,0:T(8,128)} %potentials.5) | copy-start | bytes 12582916
  3.0 6.4 %copy-start = (f32[4,32,64,256]{3,2,1,0:T(8,128)S(1)}, f32[4,32,64,256]{3,2,1,0:T(8,128)}, u32[]{:S(2)}) copy-start(f32[4,32,64,256]{3,2,1,0:T(8,128)} %orbitals.5) | copy-start | bytes 25165828
  5.2 26.7 %collective-permute-start.3 = (f32[7,32,3,256]{3,1,2,0:T(8,128)S(1)}, f32[7,32,3,256]{3,1,2,0:T(8,128)S(1)}, u32[]{:S(2)}, u32[]{:S(2)}) collective-permute-start(f32[7,32,3,256]{3,1,2,0:T(8,128)S(1)} %pad_maximum_fusion.1), channel_id=1, source_target_pairs={{0,1},{1,2},{2,3},{3,4},{4,5},{5,6},{6,7},{8,9},{9,10},{10,11},{11... | collective-permute-start | bytes 2064392 | tf_op jit(solution)/shard_map/ppermute | solution.py:353
  8.0 7.5 %copy-start.6 = (f32[4]{0:T(128)S(1)}, f32[4]{0:T(128)}, u32[]{:S(2)}) copy-start(f32[4]{0:T(128)} %param.11) | copy-start | bytes 52
  8.0 25.8 %collective-permute-start.4 = (f32[7,32,3,256]{3,1,2,0:T(8,128)S(1)}, f32[7,32,3,256]{3,1,2,0:T(8,128)S(1)}, u32[]{:S(2)}, u32[]{:S(2)}) collective-permute-start(f32[7,32,3,256]{3,1,2,0:T(8,128)S(1)} %pad_maximum_fusion.2), channel_id=1, source_target_pairs={{1,0},{2,1},{3,2},{4,3},{5,4},{6,5},{7,6},{9,8},{10,9},{11,10},{12... | collective-permute-start | bytes 2064392 | tf_op jit(solution)/shard_map/ppermute | solution.py:354
  12.3 5.3 %collective-permute-start = (f32[12,128]{1,0:T(8,128)S(1)}, f32[12,128]{1,0:T(8,128)S(1)}, u32[]{:S(2)}, u32[]{:S(2)}) collective-permute-start(f32[12,128]{1,0:T(8,128)S(1)} %reduce_sum.9), channel_id=1, source_target_pairs={{0,1},{1,0},{2,3},{3,2},{4,5},{5,4},{6,7},{7,6},{8,9},{9,8},{10,11... | collective-permute-start | bytes 18440 | tf_op jit(solution)/shard_map/ppermute | solution.py:333
  17.6 10.0 %collective-permute-start.1 = (f32[12,128]{1,0:T(8,128)S(1)}, f32[12,128]{1,0:T(8,128)S(1)}, u32[]{:S(2)}, u32[]{:S(2)}) collective-permute-start(f32[12,128]{1,0:T(8,128)S(1)} %add.134), channel_id=1, source_target_pairs={{0,2},{1,3},{2,0},{3,1},{4,6},{5,7},{6,4},{7,5},{8,10},{9,11},{10,... | collective-permute-start | bytes 18440 | tf_op jit(solution)/shard_map/ppermute | solution.py:333
  27.7 3.7 %collective-permute-start.2 = (f32[12,128]{1,0:T(8,128)S(1)}, f32[12,128]{1,0:T(8,128)S(1)}, u32[]{:S(2)}, u32[]{:S(2)}) collective-permute-start(f32[12,128]{1,0:T(8,128)S(1)} %add.135), channel_id=1, source_target_pairs={{0,4},{1,5},{2,6},{3,7},{4,0},{5,1},{6,2},{7,3},{8,12},{9,13},{10,... | collective-permute-start | bytes 18440 | tf_op jit(solution)/shard_map/ppermute | solution.py:333
  69.7 43.6 %copy-start.4 = (f32[1,256,1024]{2,1,0:T(8,128)S(1)}, f32[1,256,1024]{2,1,0:T(8,128)}, u32[]{:S(2)}) copy-start(f32[1,256,1024]{2,1,0:T(8,128)} %get-tuple-element.12) | copy-start | bytes 3145732
  69.7 43.6 %collective-permute-start.5 = (f32[1,256,1024]{2,1,0:T(8,128)}, f32[1,256,1024]{2,1,0:T(8,128)S(1)}, u32[]{:S(2)}, u32[]{:S(2)}) collective-permute-start(f32[1,256,1024]{2,1,0:T(8,128)} %get-tuple-element.12), channel_id=1, source_target_pairs={{0,8},{24,16},{1,9},{25,17},{2,10},{26,18},{3,11},{27,19},{4,12},{... | collective-permute-start | bytes 3145736 | tf_op jit(solution)/shard_map/ppermute | solution.py:403
  111.8 19.8 %copy-start.3 = (f32[1,256,1024]{2,1,0:T(8,128)S(1)}, f32[1,256,1024]{2,1,0:T(8,128)}, u32[]{:S(2)}) copy-start(f32[1,256,1024]{2,1,0:T(8,128)} %get-tuple-element.15) | copy-start | bytes 3145732
  111.8 19.8 %collective-permute-start.8 = (f32[1,256,1024]{2,1,0:T(8,128)}, f32[1,256,1024]{2,1,0:T(8,128)S(1)}, u32[]{:S(2)}, u32[]{:S(2)}) collective-permute-start(f32[1,256,1024]{2,1,0:T(8,128)} %get-tuple-element.15), channel_id=1, source_target_pairs={{0,8},{24,16},{1,9},{25,17},{2,10},{26,18},{3,11},{27,19},{4,12},{... | collective-permute-start | bytes 3145736 | tf_op jit(solution)/shard_map/ppermute | solution.py:403
  113.5 19.0 %copy-start.5 = (f32[1,256,512]{2,1,0:T(8,128)S(1)}, f32[1,256,512]{2,1,0:T(8,128)}, u32[]{:S(2)}) copy-start(f32[1,256,512]{2,1,0:T(8,128)} %get-tuple-element.13) | copy-start | bytes 1572868
  113.5 18.9 %collective-permute-start.6 = (f32[1,256,1024]{2,1,0:T(8,128)S(1)}, f32[1,256,1024]{2,1,0:T(8,128)S(1)}, u32[]{:S(2)}, u32[]{:S(2)}) collective-permute-start(f32[1,256,1024]{2,1,0:T(8,128)S(1)} %add.141), channel_id=1, source_target_pairs={{8,16},{16,8},{9,17},{17,9},{10,18},{18,10},{11,19},{19,11},{12,20... | collective-permute-start | bytes 3145736 | tf_op jit(solution)/shard_map/ppermute | solution.py:404
  131.7 6.8 %collective-permute-start.9 = (f32[1,256,1024]{2,1,0:T(8,128)S(1)}, f32[1,256,1024]{2,1,0:T(8,128)S(1)}, u32[]{:S(2)}, u32[]{:S(2)}) collective-permute-start(f32[1,256,1024]{2,1,0:T(8,128)S(1)} %add.162), channel_id=1, source_target_pairs={{8,16},{16,8},{9,17},{17,9},{10,18},{18,10},{11,19},{19,11},{12,20... | collective-permute-start | bytes 3145736 | tf_op jit(solution)/shard_map/ppermute | solution.py:404
  133.3 25.6 %collective-permute-start.7 = (f32[1,256,512]{2,1,0:T(8,128)}, f32[1,256,512]{2,1,0:T(8,128)}, u32[]{:S(2)}, u32[]{:S(2)}) collective-permute-start(f32[1,256,512]{2,1,0:T(8,128)} %slice_add_fusion.2), channel_id=1, source_target_pairs={{0,8},{8,0},{16,24},{24,16},{1,9},{9,1},{17,25},{25,17},{2,10},{10... | collective-permute-start | bytes 1572872 | tf_op jit(solution)/shard_map/ppermute | solution.py:407
  139.6 27.4 %collective-permute-start.10 = (f32[1,256,512]{2,1,0:T(8,128)S(1)}, f32[1,256,512]{2,1,0:T(8,128)}, u32[]{:S(2)}, u32[]{:S(2)}) collective-permute-start(f32[1,256,512]{2,1,0:T(8,128)S(1)} %slice_add_fusion), channel_id=1, source_target_pairs={{0,8},{8,0},{16,24},{24,16},{1,9},{9,1},{17,25},{25,17},{2,10},{10... | collective-permute-start | bytes 1572872 | tf_op jit(solution)/shard_map/ppermute | solution.py:407
  161.1 13.2 %all-to-all-start = ((f32[8,32,512]{2,1,0:T(8,128)}), f32[8,32,512]{2,1,0:T(8,128)S(1)}, u32[]{:S(2)}, u32[]{:S(2)}) async-start(f32[8,32,512]{2,1,0:T(8,128)} %bitcast.8), calls=%async_computation | async-start | bytes 1048576 | tf_op jit(solution)/shard_map/all_to_all | solution.py:412
  164.6 13.5 %copy-start.2 = (bf16[2,512,512]{2,1,0:T(8,128)(2,1)S(1)}, bf16[2,512,512]{2,1,0:T(8,128)(2,1)}, u32[]{:S(2)}) copy-start(bf16[2,512,512]{2,1,0:T(8,128)(2,1)} %constant.74.clone.table) | copy-start | bytes 3145732
  174.3 13.2 %all-to-all-start.1 = ((f32[8,32,512]{2,1,0:T(8,128)}), f32[8,32,512]{2,1,0:T(8,128)S(1)}, u32[]{:S(2)}, u32[]{:S(2)}) async-start(f32[8,32,512]{2,1,0:T(8,128)} %bitcast.10), calls=%async_computation.1 | async-start | bytes 1048576 | tf_op jit(solution)/shard_map/all_to_all | solution.py:412

commit v2 on v1

v2 whole, which is shorter than its diff:
```python
import functools

import jax
import jax.numpy as jnp
import numpy as np
from jax import lax
from jax.experimental import pallas as pl
from jax.experimental.pallas import tpu as pltpu
from jax.sharding import PartitionSpec as P

SWEEPS = 3
HALO = SWEEPS
TILE = 8
LANES = 128

spread_half = 3.5
screening = 0.25


def sine_values(length):
    index = np.arange(1, length + 1)
    phase = index[:, None] * index[None, :] % (2 * (length + 1))
    return np.sqrt(2.0 / (length + 1)) * np.sin(np.pi * phase / (length + 1))


def two_parts(values):
    whole = np.asarray(values, np.float32)
    high = whole.astype(jnp.bfloat16)
    low = (whole - high.astype(np.float32)).astype(jnp.bfloat16)
    return np.stack([high, low])


def split(value):
    high = value.astype(jnp.bfloat16)
    low = (value - high.astype(jnp.float32)).astype(jnp.bfloat16)
    return high, low


def product(a, b, contract):
    dims = (contract, ((), ()))
    dot = functools.partial(lax.dot_general, dimension_numbers=dims, preferred_element_type=jnp.float32)
    return dot(a[0], b[0]) + dot(a[1], b[0]) + dot(a[0], b[1])


def coulomb(z_index, x_index, y_index, sizes):
    nz, nx, ny = sizes
    wave_z = jnp.pi * (z_index.astype(jnp.float32) + 1.0) / (nz + 1)
    wave_x = jnp.pi * (x_index.astype(jnp.float32) + 1.0) / (nx + 1)
    wave_y = jnp.pi * (y_index.astype(jnp.float32) + 1.0) / (ny + 1)
    total = (
        wave_z[:, None, None] * wave_z[:, None, None]
        + wave_x[None, :, None] * wave_x[None, :, None]
    )
    total = total + wave_y[None, None, :] * wave_y[None, None, :] + screening
    return jnp.sqrt(4.0 * jnp.pi / total)


def project_kernel(orbitals, potentials, earlier, sums):
    count, planes, rows, width = orbitals.shape
    npot = potentials.shape[0]
    halves = width // LANES

    @pl.when(pl.program_id(0) == 0)
    def _():
        sums[...] = jnp.zeros_like(sums)

    def fold(value):
        return jnp.sum(value.reshape(rows // TILE, TILE, LANES), axis=0)

    def body(z, _):
        for half in range(halves):
            lanes = slice(half * LANES, (half + 1) * LANES)
            potential = [potentials[p, z, :, lanes] for p in range(npot)]
            for n in range(count):
                value = orbitals[n, z, :, lanes]
                square = value * value
                for p in range(npot):
                    sums[p * count + n] += fold(potential[p] * square)
                sums[npot * count + n] += fold(square)
        return 0

    lax.fori_loop(0, planes, body, 0)

    @pl.when(pl.program_id(0) == pl.num_programs(0) - 1)
    def _():
        sums[:, 0, :] = jnp.sum(sums[...], axis=1)


def project(orbitals, potentials, earlier):
    count, planes, rows, width = orbitals.shape
    npot = potentials.shape[0]
    step = 4
    total = (npot + 1) * count
    sums = pl.pallas_call(
        project_kernel,
        grid=(planes // step,),
        in_specs=[
            pl.BlockSpec((count, step, rows, width), lambda i: (0, i, 0, 0)),
            pl.BlockSpec((npot, step, rows, width), lambda i: (0, i, 0, 0)),
            pl.BlockSpec(memory_space=pl.ANY),
        ],
        out_specs=pl.BlockSpec((total, TILE, LANES), lambda i: (0, 0, 0)),
        out_shape=jax.ShapeDtypeStruct((total, TILE, LANES), jnp.float32),
        compiler_params=pltpu.CompilerParams(vmem_limit_bytes=60 << 20),
    )(orbitals, potentials, earlier)
    return sums[:, 0, :]


def edges_kernel(orbitals, potentials, local, first, last, tiles, sems):
    fields = []
    for source in (orbitals, potentials):
        fields += [source.at[i] for i in range(source.shape[0])]
    fields.append(local)
    planes, rows, width = local.shape
    copies = []
    for side, begin in enumerate((0, rows - TILE)):
        for i, field in enumerate(fields):
            copy = pltpu.make_async_copy(
                field.at[:, pl.ds(begin, TILE), :], tiles.at[side, i], sems.at[side, i]
            )
            copy.start()
            copies.append(copy)
    for copy in copies:
        copy.wait()
    for side, (out, begin) in enumerate(((first, 0), (last, TILE - HALO))):
        for i in range(len(fields)):
            for z in range(planes):
                out[i, z * HALO:(z + 1) * HALO, :] = tiles[side, i, z, begin:begin + HALO, :]


def pack_edges(orbitals, potentials, local):
    planes, _, width = local.shape
    fields = orbitals.shape[0] + potentials.shape[0] + 1
    vmem = pl.BlockSpec(memory_space=pltpu.VMEM)
    edge = jax.ShapeDtypeStruct((fields, planes * HALO, width), jnp.float32)
    return pl.pallas_call(
        edges_kernel,
        in_specs=[pl.BlockSpec(memory_space=pl.ANY)] * 3,
        out_specs=[vmem] * 2,
        out_shape=[edge] * 2,
        scratch_shapes=[
            pltpu.VMEM((2, fields, planes, TILE, width), jnp.float32),
            pltpu.SemaphoreType.DMA((2, fields)),
        ],
        compiler_params=pltpu.CompilerParams(vmem_limit_bytes=60 << 20),
    )(orbitals, potentials, local)


def stencil_kernel(
    geometry,
    coefficients, constants, place_index, z_tables, x_table,
    orbitals, potentials, local, low, high,
    mine, partner, far,
    orb, pot, loc, src, one, two, density, spectrum, low_rows, high_rows, z_table, table_sem, sems,
):
    pots, count, start, rows, strip, group = geometry
    npot = len(pots)
    planes = local.shape[0]
    width = local.shape[2]
    halves = width // LANES
    padded = rows + 2 * TILE
    wide = rows + TILE
    steps = planes // group
    f32 = jnp.float32
    begin, end = max(start - TILE, 0), min(start + rows + TILE, strip)
    place = begin - (start - TILE)
    need_low, need_high = start < TILE, start + rows + TILE > strip
    all_pots = low.shape[0] - count - 1
    packed = ((low, low_rows, TILE - HALO, need_low), (high, high_rows, padded - TILE, need_high))

    def pieces(kind, index, act):
        source, target, halo, sem = {
            "orb": (orbitals, orb, 0, 0), "pot": (potentials, pot, count, count), "loc": (local, loc, None, count + npot),
        }[kind]
        if kind == "loc":
            field, into, row, slot = source, lambda half: target.at[half], count + all_pots, sem
        elif kind == "pot":
            field, into, row, slot = source.at[pots[index]], lambda half: target.at[half, index], halo + pots[index], sem + index
        else:
            field, into, row, slot = source.at[index], lambda half: target.at[half, index], index, index
        for half in range(halves):
            lanes = pl.ds(half * LANES, LANES)
            copies = [(field.at[:, pl.ds(begin, end - begin), lanes], into(half).at[:, pl.ds(place, end - begin), :])]
            for sent, held, begin_row, needed in packed:
                if needed:
                    copies.append((sent.at[row, :, lanes], held.at[half, row]))
            for i, (a, b) in enumerate(copies):
                act(pltpu.make_async_copy(a, b, sems.at[slot, half, i]))
        if act is end_copy:
            for sent, held, begin_row, needed in packed:
                if needed:
                    for half in range(halves):
                        value = held[half, row]
                        for z in range(planes):
                            into(half)[z, begin_row:begin_row + HALO, :] = value[z * HALO:(z + 1) * HALO]

    def begin_copy(copy):
        copy.start()

    def end_copy(copy):
        copy.wait()

    pieces("loc", 0, begin_copy)
    for p in range(npot):
        pieces("pot", p, begin_copy)
    for n in range(count):
        pieces("orb", n, begin_copy)
    band = place_index[2]
    table_copy = pltpu.make_async_copy(z_tables.at[band], z_table, table_sem)
    table_copy.start()

    for field in (src, one, two):
        for p in range(npot):
            for half in range(halves):
                for z in (0, planes + 1):
                    field[half, p, z] = jnp.zeros(field.shape[3:], f32)

    def empty(z, _):
        for half in range(halves):
            for p in range(npot):
                density[half, p, z] = jnp.zeros((rows, LANES), f32)
        return 0

    lax.fori_loop(0, planes, empty, 0)
    first_edge = (place_index[0] == 1) if start == 0 else None
    last_edge = (place_index[1] == 1) if start + rows == strip else None

    pieces("loc", 0, end_copy)

    def weights(z, _):
        for half in range(halves):
            loc[half, z] = 1.0 - 2.0 * loc[half, z]
        return 0

    lax.fori_loop(0, planes, weights, 0)
    for p in range(npot):
        pieces("pot", p, end_copy)

    def cut(size):
        most = 3 * TILE if size % (3 * TILE) == 0 else 2 * TILE
        return [(r, min(most, size - r)) for r in range(0, size, most)]

    def sides(center):
        lane = lax.broadcasted_iota(jnp.int32, center[0].shape, 1)
        down = [pltpu.roll(c, 1, 1) for c in center]
        up = [pltpu.roll(c, LANES - 1, 1) for c in center]
        zero = jnp.zeros_like(center[0])
        down = [jnp.where(lane == 0, before, now) for before, now in zip([zero] + down[:-1], down)]
        up = [jnp.where(lane == LANES - 1, after, now) for after, now in zip(up[1:] + [zero], up)]
        return [a + b for a, b in zip(down, up)]

    def apply(field, offset, size, loc_offset, finish, step):
        z0 = step * group
        for r, length in cut(size):
            def load(p, i, shift):
                return [field[h, p, z0 + i + 1, pl.ds(offset + r + shift, length), :] for h in range(halves)]

            before = [load(p, -1, 0) for p in range(npot)]
            center = [load(p, 0, 0) for p in range(npot)]
            beside = [sides(c) for c in center]
            for i in range(group):
                after = [load(p, i + 1, 0) for p in range(npot)]
                beside_after = [sides(c) for c in after] if i + 1 < group else None
                total = []
                for p in range(npot):
                    under, over = load(p, i, -1), load(p, i, 1)
                    total.append([
                        (before[p][h] + after[p][h]) + (under[h] + over[h]) + beside[p][h] for h in range(halves)
                    ])
                for h in range(halves):
                    weight = loc[h, z0 + i, pl.ds(loc_offset + r, length), :]
                    finish(h, z0 + i, r, length, [t[h] for t in total], [c[h] for c in center], weight)
                before, center, beside = center, after, beside_after

    def clear(field, where, row, size):
        if where is not None:
            @pl.when(where)
            def _():
                for h in range(halves):
                    for p in range(npot):
                        field[h, p, :, pl.ds(row, size), :] = jnp.zeros((planes + 2, size, LANES), f32)

    def orbital(n, _):
        pieces("orb", n, end_copy)

        alpha, beta, scale = (constants[n, i] for i in range(3))
        factor = [coefficients[pots[p] * count + n] for p in range(npot)]

        def source(step):
            for i in range(group):
                z = step * group + i
                for h in range(halves):
                    value = orb[h, n, z]
                    for p in range(npot):
                        src[h, p, z + 1] = (pot[h, p, z] - factor[p]) * value

        def finish_one(h, z, r, length, total, center, weight):
            weight = weight + alpha
            for p in range(npot):
                one[h, p, z + 1, pl.ds(r, length), :] = total[p] + weight * center[p]

        def finish_two(h, z, r, length, total, center, weight):
            for p in range(npot):
                two[h, p, z + 1, pl.ds(r, length), :] = total[p] + weight * center[p]

        def finish_three(h, z, r, length, total, center, weight):
            value = orb[h, n, z, pl.ds(TILE + r, length), :] * scale
            for p in range(npot):
                third = total[p] + weight * center[p] + beta * one[h, p, z + 1, pl.ds(2 + r, length), :]
                density[h, p, z, pl.ds(r, length), :] += third * value

        applies = [
            source,
            functools.partial(apply, src, TILE - 2, wide, TILE - 2, finish_one),
            functools.partial(apply, one, 1, wide, TILE - 1, finish_two),
            functools.partial(apply, two, 1, rows, TILE, finish_three),
        ]
        for position, work in enumerate(applies):
            def body(step, _, work=work):
                work(step)
                return 0

            lax.fori_loop(0, steps, body, 0)
            if position == 1:
                clear(one, first_edge, 0, 2)
                clear(one, last_edge, rows + 2, 2)
            if position == 2:
                clear(two, first_edge, 0, 1)
                clear(two, last_edge, rows + 1, 1)
        return 0

    lax.fori_loop(0, count, orbital, 0)

    table_copy.wait()
    z_parts = (z_table[0], z_table[1])
    x_parts = (x_table[0], x_table[1])
    share = mine.shape[1] // npot
    block = min(share, 2 * LANES)
    for p in range(npot):
        for tile in range(rows // TILE):
            span = pl.ds(tile * TILE, TILE)
            value = jnp.concatenate(
                [density[h, p, :, span, :].reshape(planes * TILE, LANES) for h in range(halves)], axis=-1
            )
            value = product(z_parts, split(value), ((1,), (0,)))
            spectrum[:, span, :] = value.reshape(planes, TILE, width)
        for piece in range(planes * rows // block):
            at = piece * block
            value = spectrum[at // rows:(at + block) // rows].reshape(block, width)
            value = product(x_parts, split(value), ((1,), (1,)))
            for out, low_end, high_end in ((mine, 0, share), (partner, share, 2 * share)):
                if low_end <= at < high_end:
                    out[:, p * share + at - low_end:p * share + at - low_end + block] = value
            if at >= 2 * share:
                part, at = divmod(at - 2 * share, share)
                column = (part * npot + p) * share + at
                far[:, column:column + block] = value


def stencil(pots, start, rows, group, coefficients, constants, edges, tables, fields, halos):
    orbitals, potentials, local = fields
    count, planes, strip, width = orbitals.shape
    halves = width // LANES
    npot = len(pots)
    padded = rows + 2 * TILE
    share = planes * rows // 4
    geometry = (pots, count, start, rows, strip, group)
    vmem = pl.BlockSpec(memory_space=pltpu.VMEM)
    smem = pl.BlockSpec(memory_space=pltpu.SMEM)
    anywhere = pl.BlockSpec(memory_space=pl.ANY)
    f32 = jnp.float32
    return pl.pallas_call(
        functools.partial(stencil_kernel, geometry),
        in_specs=[smem, smem, smem, anywhere, vmem] + [anywhere] * 5,
        out_specs=[vmem] * 3,
        out_shape=[
            jax.ShapeDtypeStruct((width, npot * share), f32),
            jax.ShapeDtypeStruct((width, npot * share), f32),
            jax.ShapeDtypeStruct((width, npot * 2 * share), f32),
        ],
        scratch_shapes=[
            pltpu.VMEM((halves, count, planes, padded, LANES), f32),
            pltpu.VMEM((halves, npot, planes, padded, LANES), f32),
            pltpu.VMEM((halves, planes, padded, LANES), f32),
            pltpu.VMEM((halves, npot, planes + 2, padded, LANES), f32),
            pltpu.VMEM((halves, npot, planes + 2, padded, LANES), f32),
            pltpu.VMEM((halves, npot, planes + 2, padded, LANES), f32),
            pltpu.VMEM((halves, npot, planes, rows, LANES), f32),
            pltpu.VMEM((planes, rows, width), f32),
            pltpu.VMEM((halves, *halos[0].shape[:2], LANES), f32),
            pltpu.VMEM((halves, *halos[0].shape[:2], LANES), f32),
            pltpu.VMEM(tables[0].shape[1:], jnp.bfloat16),
            pltpu.SemaphoreType.DMA(()),
            pltpu.SemaphoreType.DMA((1 + npot + count, halves, 3)),
        ],
        compiler_params=pltpu.CompilerParams(vmem_limit_bytes=60 << 20),
        cost_estimate=pl.CostEstimate(flops=1 << 34, bytes_accessed=64 << 20, transcendentals=0),
    )(coefficients, constants, edges, *tables, orbitals, potentials, local, *halos)


def finish_kernel(received, table, weight, out):
    parts, x_share, lanes = received.shape
    z_share = out.shape[0]
    strip = lanes // z_share
    table_parts = (table[0], table[1])
    lane = lax.broadcasted_iota(jnp.int32, (x_share, LANES), 1)
    lower = lane < strip
    for pair in range(z_share // 2):
        columns = slice(pair * LANES, (pair + 1) * LANES)
        blocks = [received[i, :, columns] for i in range(parts)]
        rolled = [pltpu.roll(b, strip, 1) for b in blocks]
        even = [jnp.where(lower, blocks[i], rolled[i + 1]) for i in range(0, parts, 2)]
        odd = [jnp.where(lower, rolled[i], blocks[i + 1]) for i in range(0, parts, 2)]
        both = jnp.concatenate([jnp.concatenate(even, axis=-1), jnp.concatenate(odd, axis=-1)], axis=0)
        value = product(split(both), table_parts, ((1,), (0,)))
        out[2 * pair] = value[:x_share] * weight[2 * pair]
        out[2 * pair + 1] = value[x_share:] * weight[2 * pair + 1]


def finish(received, table, weight):
    vmem = pl.BlockSpec(memory_space=pltpu.VMEM)
    return pl.pallas_call(
        finish_kernel,
        in_specs=[vmem] * 3,
        out_specs=vmem,
        out_shape=jax.ShapeDtypeStruct(weight.shape, jnp.float32),
        compiler_params=pltpu.CompilerParams(vmem_limit_bytes=40 << 20),
    )(received, table, weight)


def total_over(values, axis):
    count = lax.axis_size(axis)
    step = 1
    while step < count:
        values = values + lax.ppermute(values, axis, [(i, i ^ step) for i in range(count)])
        step *= 2
    return values


def per_device(orbitals, potentials, local_potential, shifts):
    f32 = jnp.float32
    count, nz, strip, nx = orbitals.shape
    npot = potentials.shape[0]
    gy, bands = lax.axis_size("gy"), lax.axis_size("band")
    ny = strip * gy
    band, place = lax.axis_index("band"), lax.axis_index("gy")
    z_share, x_share = nz // bands, nx // gy

    first, last = pack_edges(orbitals, potentials, local_potential)
    forward = [(i, i + 1) for i in range(gy - 1)]
    backward = [(b, a) for a, b in forward]
    halos = (lax.ppermute(last, "gy", forward), lax.ppermute(first, "gy", backward))
    sums = total_over(project(orbitals, potentials, first), "gy")
    fields = (orbitals, potentials, local_potential)
    totals = jnp.sum(sums, axis=1).reshape(npot + 1, count)
    coefficients = (totals[:npot] / totals[npot]).reshape(-1)

    excess = shifts / spread_half
    s = 1.0 + excess
    less_one = excess * (2.0 + excess)
    fourth = 1.0 + 8.0 * s * s * less_one
    unit = 2.0 * spread_half
    constants = jnp.stack([unit * s, unit * unit * less_one, -32.0 / (spread_half * unit**3) / fourth], axis=1)
    edges = jnp.stack([(place == 0).astype(jnp.int32), (place == gy - 1).astype(jnp.int32), band])

    sine_z = sine_values(nz)
    paired = bands == 4
    if paired:
        orders = [[b, b ^ 1] + ([2, 3] if b < 2 else [1, 0]) for b in range(bands)]
    else:
        orders = [list(range(bands))] * bands
    by_band = []
    for order in orders:
        index = np.concatenate([np.arange(z_share) + z_share * o for o in order])
        by_band.append(two_parts(np.kron(sine_z[index], np.eye(TILE))))
    z_table = jnp.asarray(np.stack(by_band))
    tables = (z_table, jnp.asarray(two_parts(sine_values(nx))))
    z_index = band * z_share + jnp.arange(z_share, dtype=jnp.int32)
    x_index = place * x_share + jnp.arange(x_share, dtype=jnp.int32)
    weight = coulomb(z_index, x_index, jnp.arange(ny, dtype=jnp.int32), (nz, nx, ny))

    sine_y = sine_values(ny)
    y_table = jnp.asarray(two_parts(sine_y))
    outs = []
    for p in range(npot):
        mine, partner, far = stencil(
            (p,), 0, strip, 16, coefficients, constants, edges, tables, fields, halos
        )
        share = mine.shape[1]
        if paired:
            inward = lax.ppermute(far, "band", [(0, 1), (3, 2)])
            swapped = lax.ppermute(partner, "band", [(0, 1), (1, 0), (2, 3), (3, 2)])
            close = far[:, :share] + inward[:, :share]
            distant = far[:, share:] + inward[:, share:]
            close = lax.ppermute(close, "band", [(1, 2), (2, 1)])
            distant = lax.ppermute(distant, "band", [(1, 3), (2, 0)])
            total = mine + swapped + (close + distant)
        else:
            joined = jnp.concatenate([mine, partner, far], axis=1)
            total = lax.psum_scatter(joined, "band", scatter_dimension=1, tiled=True)
        spread = total.reshape(gy, x_share, -1)
        received = lax.all_to_all(spread, "gy", split_axis=0, concat_axis=0, tiled=True)
        if paired and 2 * strip == LANES:
            outs.append(finish(received, y_table, weight))
        else:
            terms = received.reshape(gy, x_share, z_share, strip)
            table = jnp.asarray(sine_y, f32).reshape(gy, strip, ny)
            value = jnp.einsum("sjky,sym->kjm", terms, table, precision=lax.Precision.HIGHEST)
            outs.append(value * weight)
    return jnp.stack(outs)


def solution(mesh):
    placed = (
        P("band", None, "gy", None),
        P(None, None, "gy", None),
        P(None, "gy", None),
        P("band"),
    )
    return jax.shard_map(
        per_device,
        mesh=mesh,
        in_specs=placed,
        out_specs=P(None, "band", "gy", None),
        check_vma=False,
    )
```

time: 190 us -> 156 us (0.82)
  Pallas kernels: 77.7 us -> 63 us
  local copies, waits for them, and re-layouts: 11.1 us -> 2.99 us
  waiting for transfers between devices: 43.5 us -> 35.7 us
  starting transfers between devices: 47.2 us -> 41.9 us
    pallas_call x2 -> x3, Pallas kernels: 72.3 us -> 52.6 us  [the longest x2 49 us: stencil(): pl.pallas_call(functools.partial(stencil_kernel, geometry), in_specs=[sme...]
    ppermute x8 -> x10, starting transfers between devices: 35.2 us -> 18.3 us  [the longest x2 5.65 us: per_device(): swapped = lax.ppermute(partner, 'band', [(0, 1), (1, 0), (2, 3), (3, 2)])]
    all_to_all x2, starting transfers between devices: 6.99 us -> 16.7 us  [per_device(): lax.all_to_all(spread, 'gy', split_axis=0, concat_axis=0, tiled=True)]
    ppermute x3, waiting for transfers between devices: 10.8 us -> 2.03 us  [total_over(): lax.ppermute(values, axis, [(i, i ^ step) for i in range(count)])]
    pallas_call x1, Pallas kernels: 2.88 us -> 7.88 us  [project(): pl.pallas_call(project_kernel, grid=(planes // step,), in_specs=[pl.Block...]
    pad x2 -> x0, local copies, waits for them, and re-layouts: 2.86 us -> none  [the longest x1 1.46 us: per_device(): low = jnp.pad(low, ((0, 0), (0, 0), (TILE - HALO, 0), (0, 0)))]
    all_to_all x2, waiting for transfers between devices: 13.3 us -> 15.3 us  [per_device(): lax.all_to_all(spread, 'gy', split_axis=0, concat_axis=0, tiled=True)]
    ppermute x3, starting transfers between devices: 4.96 us -> 6.98 us  [total_over(): lax.ppermute(values, axis, [(i, i ^ step) for i in range(count)])]
  transfers between devices with their start and end apart: 13 -> 15, of which waited for: 6 -> 7; matrix products, arithmetic and copies ran while one was open for 7% -> 7% of each run, Pallas kernels for 22% -> 22%
where the time goes in v2:
time: 156 us; the launch traced here: 155 us
  Pallas kernels  63 us (40%)
  starting transfers between devices  41.9 us (27%)
  waiting for transfers between devices  35.7 us (23%)
  other arithmetic  11.5 us (7%)
  local copies, waits for them, and re-layouts  2.99 us (2%)
    pallas_call x2, Pallas kernels, stencil(): pl.pallas_call(functools.partial(stencil_kernel, geometry), in_specs=[sme...  49 us
    all_to_all x2, starting transfers between devices, per_device(): lax.all_to_all(spread, 'gy', split_axis=0, concat_axis=0, tiled=True)  16.7 us
    all_to_all x2, waiting for transfers between devices, per_device(): lax.all_to_all(spread, 'gy', split_axis=0, concat_axis=0, tiled=True)  15.3 us
    ppermute x2, waiting for transfers between devices, per_device(): inward = lax.ppermute(far, 'band', [(0, 1), (3, 2)])  9.86 us
    ppermute x2, waiting for transfers between devices, per_device(): swapped = lax.ppermute(partner, 'band', [(0, 1), (1, 0), (2, 3), (3, 2)])  8.03 us
    pallas_call x1, Pallas kernels, project(): pl.pallas_call(project_kernel, grid=(planes // step,), in_specs=[pl.Block...  7.88 us
    ppermute x3, starting transfers between devices, total_over(): lax.ppermute(values, axis, [(i, i ^ step) for i in range(count)])  6.98 us
    ppermute x2, starting transfers between devices, per_device(): swapped = lax.ppermute(partner, 'band', [(0, 1), (1, 0), (2, 3), (3, 2)])  5.65 us
  transfers between devices with their start and end apart: 15, of which 7 were waited for; matrix products, arithmetic and copies ran while one was open for 7% of the time, Pallas kernels for 22%

profile of v2, /device:TPU:0, one launch (start us, length us, event | category | flops | bytes accessed | tf_op | source)
XLA Modules:
  0.0 155.3 jit_solution(962313852655387109)
XLA Ops:
  0.0 3.6 %shard_map.73 = (f32[7,96,256]{2,1,0:T(8,128)}, f32[7,96,256]{2,1,0:T(8,128)}) custom-call(f32[4,32,64,256]{3,2,1,0:T(8,128)} %orbitals.7, f32[2,32,64,256]{3,2,1,0:T(8,128)} %potentials.7, f32[32,64,256]{2,1,0:T(8,128)} %local.5), custom_call_target="tpu_custom_call" | custom-call | tf_op jit(solution)/shard_map/pallas_call | solution.py:136
  3.6 1.4 collective-permute-start.4
  5.1 7.9 %shard_map.74 = f32[12,8,128]{2,1,0:T(8,128)} custom-call(f32[4,32,64,256]{3,2,1,0:T(8,128)} %orbitals.7, f32[2,32,64,256]{3,2,1,0:T(8,128)} %potentials.7, f32[7,96,256]{2,1,0:T(8,128)} %get-tuple-element.13.earlier), custom_call_target="tpu_custom_call" | custom-call | tf_op jit(solution)/shard_map/pallas_call | solution.py:94
  14.9 2.0 %collective-permute-start.3 = (f32[7,96,256]{2,1,0:T(8,128)S(1)}, f32[7,96,256]{2,1,0:T(8,128)S(1)}, u32[]{:S(2)}, u32[]{:S(2)}) collective-permute-start(f32[7,96,256]{2,1,0:T(8,128)S(1)} %copy-done.6), channel_id=1, source_target_pairs={{0,1},{1,2},{2,3},{3,4},{4,5},{5,6},{6,7},{8,9},{9,10},{10,11},{11... | collective-permute-start | bytes 2064392 | tf_op jit(solution)/shard_map/ppermute | solution.py:452
  17.2 3.0 %collective-permute-start.1 = (f32[12,128]{1,0:T(8,128)S(1)}, f32[12,128]{1,0:T(8,128)S(1)}, u32[]{:S(2)}, u32[]{:S(2)}) collective-permute-start(f32[12,128]{1,0:T(8,128)S(1)} %fusion), channel_id=1, source_target_pairs={{0,2},{1,3},{2,0},{3,1},{4,6},{5,7},{6,4},{7,5},{8,10},{9,11},{10,... | collective-permute-start | bytes 18440 | tf_op jit(solution)/shard_map/ppermute | solution.py:435
  21.8 2.9 %collective-permute-start.2 = (f32[12,128]{1,0:T(8,128)S(1)}, f32[12,128]{1,0:T(8,128)S(1)}, u32[]{:S(2)}, u32[]{:S(2)}) collective-permute-start(f32[12,128]{1,0:T(8,128)S(1)} %add.133), channel_id=1, source_target_pairs={{0,4},{1,5},{2,6},{3,7},{4,0},{5,1},{6,2},{7,3},{8,12},{9,13},{10,... | collective-permute-start | bytes 18440 | tf_op jit(solution)/shard_map/ppermute | solution.py:435
  28.9 24.5 %shard_map.75 = (f32[256,512]{1,0:T(8,128)}, f32[256,512]{1,0:T(8,128)}, f32[256,1024]{1,0:T(8,128)}) custom-call(f32[8]{0:T(128)} %slice_divide_fusion.coefficients, f32[4,3]{1,0:T(4,128)} %pad_maximum_fusion.1.constants, s32[3]{0:T(128)} %pad_add_fusion.place_index, bf16[4,2,256,256]{3,2,1,0:T(8,128)(2,1)} %constant.61.clone.z_tables, ...), custom_call_target="tpu_custom_call" | custom-call | flops 17179869184 | bytes 67108864 | tf_op jit(solution)/shard_map/pallas_call | solution.py:372
  53.4 3.7 %collective-permute-start.6 = (f32[256,1024]{1,0:T(8,128)}, f32[256,1024]{1,0:T(8,128)S(1)}, u32[]{:S(2)}, u32[]{:S(2)}) collective-permute-start(f32[256,1024]{1,0:T(8,128)} %get-tuple-element.17), channel_id=1, source_target_pairs={{0,8},{24,16},{1,9},{25,17},{2,10},{26,18},{3,11},{27,19},{4,12},{... | collective-permute-start | bytes 3145736 | tf_op jit(solution)/shard_map/ppermute | solution.py:491
  57.1 24.5 %shard_map.77 = (f32[256,512]{1,0:T(8,128)}, f32[256,512]{1,0:T(8,128)}, f32[256,1024]{1,0:T(8,128)}) custom-call(f32[8]{0:T(128)} %slice_divide_fusion.coefficients, f32[4,3]{1,0:T(4,128)} %pad_maximum_fusion.1.constants, s32[3]{0:T(128)} %pad_add_fusion.place_index, bf16[4,2,256,256]{3,2,1,0:T(8,128)(2,1)} %constant.61.clone.z_tables, ...), custom_call_target="tpu_custom_call" | custom-call | flops 17179869184 | bytes 67108864 | tf_op jit(solution)/shard_map/pallas_call | solution.py:372
  81.6 1.4 collective-permute-start.10
  85.1 1.3 collective-permute-start.8
  86.4 5.6 %collective-permute-start.9 = (f32[256,512]{1,0:T(8,128)}, f32[256,512]{1,0:T(8,128)S(1)}, u32[]{:S(2)}, u32[]{:S(2)}) collective-permute-start(f32[256,512]{1,0:T(8,128)} %get-tuple-element.19), channel_id=1, source_target_pairs={{0,8},{8,0},{16,24},{24,16},{1,9},{9,1},{17,25},{25,17},{2,10},{10... | collective-permute-start | bytes 1572872 | tf_op jit(solution)/shard_map/ppermute | solution.py:492
  92.0 9.9 %collective-permute-done.10 = f32[256,1024]{1,0:T(8,128)S(1)} collective-permute-done((f32[256,1024]{1,0:T(8,128)}, f32[256,1024]{1,0:T(8,128)S(1)}, u32[]{:S(2)}, u32[]{:S(2)}) %collective-permute-start.10) | collective-permute-done | bytes 1048608 | tf_op jit(solution)/shard_map/ppermute | solution.py:491
  101.8 2.4 %slice_add_fusion = (f32[256,512]{1,0:T(8,128)}, f32[256,512]{1,0:T(8,128)}) fusion(f32[256,1024]{1,0:T(8,128)S(1)} %collective-permute-done.10, f32[256,1024]{1,0:T(8,128)} %get-tuple-element.20), kind=kLoop, calls=%fused_computation.1 | loop fusion | flops 262144 | bytes 3145728 | tf_op jit(solution)/shard_map/add | solution.py:494
  105.0 8.0 %collective-permute-done.5 = f32[256,512]{1,0:T(8,128)} collective-permute-done((f32[256,512]{1,0:T(8,128)}, f32[256,512]{1,0:T(8,128)}, u32[]{:S(2)}, u32[]{:S(2)}) %collective-permute-start.5) | collective-permute-done | bytes 524320 | tf_op jit(solution)/shard_map/ppermute | solution.py:492
  113.1 1.3 collective-permute-start.12
  114.4 2.4 %add_add_fusion.1 = f32[256,512]{1,0:T(8,128)} fusion(f32[256,512]{1,0:T(8,128)S(1)} %collective-permute-done.7, f32[256,512]{1,0:T(8,128)} %collective-permute-done.8, f32[256,512]{1,0:T(8,128)} %get-tuple-element.15, f32[256,512]{1,0:T(8,128)} %collective-permute-done.5), kind=kLoop, calls=%fused_computation.7 | loop fusion | flops 393216 | bytes 2621440 | tf_op jit(solution)/shard_map/add | solution.py:497
  116.8 12.4 %all-to-all-start = ((f32[8,32,512]{2,1,0:T(8,128)}), f32[8,32,512]{2,1,0:T(8,128)S(1)}, u32[]{:S(2)}, u32[]{:S(2)}) async-start(f32[8,32,512]{2,1,0:T(8,128)} %bitcast.6), calls=%async_computation | async-start | bytes 1048576 | tf_op jit(solution)/shard_map/all_to_all | solution.py:502
  129.7 2.1 %add_add_fusion = f32[256,512]{1,0:T(8,128)} fusion(f32[256,512]{1,0:T(8,128)S(1)} %collective-permute-done.11, f32[256,512]{1,0:T(8,128)} %collective-permute-done.12, f32[256,512]{1,0:T(8,128)S(1)} %copy-done.2, f32[256,512]{1,0:T(8,128)S(1)} %collective-permute-done.9), kind=kLoop, calls=%fused_computation.5 | loop fusion | flops 393216 | bytes 2621440 | tf_op jit(solution)/shard_map/add | solution.py:497
  131.8 7.2 %all-to-all-done.received = f32[8,32,512]{2,1,0:T(8,128)S(1)} async-done(((f32[8,32,512]{2,1,0:T(8,128)}), f32[8,32,512]{2,1,0:T(8,128)S(1)}, u32[]{:S(2)}, u32[]{:S(2)}) %all-to-all-start) | async-done | bytes 524320 | tf_op jit(solution)/shard_map/all_to_all | solution.py:502
  139.0 4.2 %all-to-all-start.1 = ((f32[8,32,512]{2,1,0:T(8,128)}), f32[8,32,512]{2,1,0:T(8,128)S(1)}, u32[]{:S(2)}, u32[]{:S(2)}) async-start(f32[8,32,512]{2,1,0:T(8,128)} %bitcast.8), calls=%async_computation.1 | async-start | bytes 1048576 | tf_op jit(solution)/shard_map/all_to_all | solution.py:502
  143.5 1.3 shard_map.76
  144.8 8.1 %all-to-all-done.1.received = f32[8,32,512]{2,1,0:T(8,128)S(1)} async-done(((f32[8,32,512]{2,1,0:T(8,128)}), f32[8,32,512]{2,1,0:T(8,128)S(1)}, u32[]{:S(2)}, u32[]{:S(2)}) %all-to-all-start.1) | async-done | bytes 524320 | tf_op jit(solution)/shard_map/all_to_all | solution.py:502
  152.9 1.3 shard_map.78
  (51 shorter events, 12.9 us)
Async XLA Ops:
  3.6 11.3 %copy-start.6 = (f32[7,96,256]{2,1,0:T(8,128)S(1)}, f32[7,96,256]{2,1,0:T(8,128)}, u32[]{:S(2)}) copy-start(f32[7,96,256]{2,1,0:T(8,128)} %get-tuple-element.14) | copy-start | bytes 2064388
  3.6 13.2 %copy-start.3 = (f32[4]{0:T(128)S(1)}, f32[4]{0:T(128)}, u32[]{:S(2)}) copy-start(f32[4]{0:T(128)} %param.10) | copy-start | bytes 52
  3.6 23.5 %collective-permute-start.4 = (f32[7,96,256]{2,1,0:T(8,128)}, f32[7,96,256]{2,1,0:T(8,128)S(1)}, u32[]{:S(2)}, u32[]{:S(2)}) collective-permute-start(f32[7,96,256]{2,1,0:T(8,128)} %get-tuple-element.13.earlier), channel_id=1, source_target_pairs={{1,0},{2,1},{3,2},{4,3},{5,4},{6,5},{7,6},{9,8},{10,9},{11,10},{12... | collective-permute-start | bytes 2064392 | tf_op jit(solution)/shard_map/ppermute | solution.py:452
  13.8 3.4 %collective-permute-start = (f32[12,128]{1,0:T(8,128)S(1)}, f32[12,128]{1,0:T(8,128)S(1)}, u32[]{:S(2)}, u32[]{:S(2)}) collective-permute-start(f32[12,128]{1,0:T(8,128)S(1)} %bitcast.20), channel_id=1, source_target_pairs={{0,1},{1,0},{2,3},{3,2},{4,5},{5,4},{6,7},{7,6},{8,9},{9,8},{10,11... | collective-permute-start | bytes 18440 | tf_op jit(solution)/shard_map/ppermute | solution.py:435
  14.9 12.3 %collective-permute-start.3 = (f32[7,96,256]{2,1,0:T(8,128)S(1)}, f32[7,96,256]{2,1,0:T(8,128)S(1)}, u32[]{:S(2)}, u32[]{:S(2)}) collective-permute-start(f32[7,96,256]{2,1,0:T(8,128)S(1)} %copy-done.6), channel_id=1, source_target_pairs={{0,1},{1,2},{2,3},{3,4},{4,5},{5,6},{6,7},{8,9},{9,10},{10,11},{11... | collective-permute-start | bytes 2064392 | tf_op jit(solution)/shard_map/ppermute | solution.py:452
  17.2 4.6 %collective-permute-start.1 = (f32[12,128]{1,0:T(8,128)S(1)}, f32[12,128]{1,0:T(8,128)S(1)}, u32[]{:S(2)}, u32[]{:S(2)}) collective-permute-start(f32[12,128]{1,0:T(8,128)S(1)} %fusion), channel_id=1, source_target_pairs={{0,2},{1,3},{2,0},{3,1},{4,6},{5,7},{6,4},{7,5},{8,10},{9,11},{10,... | collective-permute-start | bytes 18440 | tf_op jit(solution)/shard_map/ppermute | solution.py:435
  21.8 4.5 %collective-permute-start.2 = (f32[12,128]{1,0:T(8,128)S(1)}, f32[12,128]{1,0:T(8,128)S(1)}, u32[]{:S(2)}, u32[]{:S(2)}) collective-permute-start(f32[12,128]{1,0:T(8,128)S(1)} %add.133), channel_id=1, source_target_pairs={{0,4},{1,5},{2,6},{3,7},{4,0},{5,1},{6,2},{7,3},{8,12},{9,13},{10,... | collective-permute-start | bytes 18440 | tf_op jit(solution)/shard_map/ppermute | solution.py:435
  27.2 0.9 copy-start.4
  28.0 0.9 copy-start.5
  53.4 29.6 %copy-start.1 = (f32[256,1024]{1,0:T(8,128)S(1)}, f32[256,1024]{1,0:T(8,128)}, u32[]{:S(2)}) copy-start(f32[256,1024]{1,0:T(8,128)} %get-tuple-element.17) | copy-start | bytes 3145732
  53.4 29.6 %collective-permute-start.6 = (f32[256,1024]{1,0:T(8,128)}, f32[256,1024]{1,0:T(8,128)S(1)}, u32[]{:S(2)}, u32[]{:S(2)}) collective-permute-start(f32[256,1024]{1,0:T(8,128)} %get-tuple-element.17), channel_id=1, source_target_pairs={{0,8},{24,16},{1,9},{25,17},{2,10},{26,18},{3,11},{27,19},{4,12},{... | collective-permute-start | bytes 3145736 | tf_op jit(solution)/shard_map/ppermute | solution.py:491
  81.6 20.2 %collective-permute-start.10 = (f32[256,1024]{1,0:T(8,128)}, f32[256,1024]{1,0:T(8,128)S(1)}, u32[]{:S(2)}, u32[]{:S(2)}) collective-permute-start(f32[256,1024]{1,0:T(8,128)} %get-tuple-element.20), channel_id=1, source_target_pairs={{0,8},{24,16},{1,9},{25,17},{2,10},{26,18},{3,11},{27,19},{4,12},{... | collective-permute-start | bytes 3145736 | tf_op jit(solution)/shard_map/ppermute | solution.py:491
  82.9 30.1 %collective-permute-start.5 = (f32[256,512]{1,0:T(8,128)}, f32[256,512]{1,0:T(8,128)}, u32[]{:S(2)}, u32[]{:S(2)}) collective-permute-start(f32[256,512]{1,0:T(8,128)} %get-tuple-element.16), channel_id=1, source_target_pairs={{0,8},{8,0},{16,24},{24,16},{1,9},{9,1},{17,25},{25,17},{2,10},{10... | collective-permute-start | bytes 1572872 | tf_op jit(solution)/shard_map/ppermute | solution.py:492
  84.3 45.5 %copy-start.2 = (f32[256,512]{1,0:T(8,128)S(1)}, f32[256,512]{1,0:T(8,128)}, u32[]{:S(2)}) copy-start(f32[256,512]{1,0:T(8,128)} %get-tuple-element.18) | copy-start | bytes 1572868
  84.3 30.1 %collective-permute-start.7 = (f32[256,512]{1,0:T(8,128)}, f32[256,512]{1,0:T(8,128)S(1)}, u32[]{:S(2)}, u32[]{:S(2)}) collective-permute-start(f32[256,512]{1,0:T(8,128)} %get-tuple-element.22), channel_id=1, source_target_pairs={{8,16},{16,8},{9,17},{17,9},{10,18},{18,10},{11,19},{19,11},{12,20... | collective-permute-start | bytes 1572872 | tf_op jit(solution)/shard_map/ppermute | solution.py:495
  85.1 29.3 %collective-permute-start.8 = (f32[256,512]{1,0:T(8,128)}, f32[256,512]{1,0:T(8,128)}, u32[]{:S(2)}, u32[]{:S(2)}) collective-permute-start(f32[256,512]{1,0:T(8,128)} %get-tuple-element.21), channel_id=1, source_target_pairs={{8,24},{16,0},{9,25},{17,1},{10,26},{18,2},{11,27},{19,3},{12,28},... | collective-permute-start | bytes 1572872 | tf_op jit(solution)/shard_map/ppermute | solution.py:496
  86.4 42.9 %collective-permute-start.9 = (f32[256,512]{1,0:T(8,128)}, f32[256,512]{1,0:T(8,128)S(1)}, u32[]{:S(2)}, u32[]{:S(2)}) collective-permute-start(f32[256,512]{1,0:T(8,128)} %get-tuple-element.19), channel_id=1, source_target_pairs={{0,8},{8,0},{16,24},{24,16},{1,9},{9,1},{17,25},{25,17},{2,10},{10... | collective-permute-start | bytes 1572872 | tf_op jit(solution)/shard_map/ppermute | solution.py:492
  104.2 39.3 %copy-start = (bf16[2,512,512]{2,1,0:T(8,128)(2,1)S(1)}, bf16[2,512,512]{2,1,0:T(8,128)(2,1)}, u32[]{:S(2)}) copy-start(bf16[2,512,512]{2,1,0:T(8,128)(2,1)} %constant.63.clone.table) | copy-start | bytes 3145732
  104.2 25.1 %collective-permute-start.11 = (f32[256,512]{1,0:T(8,128)}, f32[256,512]{1,0:T(8,128)S(1)}, u32[]{:S(2)}, u32[]{:S(2)}) collective-permute-start(f32[256,512]{1,0:T(8,128)} %get-tuple-element.24), channel_id=1, source_target_pairs={{8,16},{16,8},{9,17},{17,9},{10,18},{18,10},{11,19},{19,11},{12,20... | collective-permute-start | bytes 1572872 | tf_op jit(solution)/shard_map/ppermute | solution.py:495
  113.1 16.7 %collective-permute-start.12 = (f32[256,512]{1,0:T(8,128)}, f32[256,512]{1,0:T(8,128)}, u32[]{:S(2)}, u32[]{:S(2)}) collective-permute-start(f32[256,512]{1,0:T(8,128)} %get-tuple-element.23), channel_id=1, source_target_pairs={{8,24},{16,0},{9,25},{17,1},{10,26},{18,2},{11,27},{19,3},{12,28},... | collective-permute-start | bytes 1572872 | tf_op jit(solution)/shard_map/ppermute | solution.py:496
  116.8 22.2 %all-to-all-start = ((f32[8,32,512]{2,1,0:T(8,128)}), f32[8,32,512]{2,1,0:T(8,128)S(1)}, u32[]{:S(2)}, u32[]{:S(2)}) async-start(f32[8,32,512]{2,1,0:T(8,128)} %bitcast.6), calls=%async_computation | async-start | bytes 1048576 | tf_op jit(solution)/shard_map/all_to_all | solution.py:502
  139.0 14.0 %all-to-all-start.1 = ((f32[8,32,512]{2,1,0:T(8,128)}), f32[8,32,512]{2,1,0:T(8,128)S(1)}, u32[]{:S(2)}, u32[]{:S(2)}) async-start(f32[8,32,512]{2,1,0:T(8,128)} %bitcast.8), calls=%async_computation.1 | async-start | bytes 1048576 | tf_op jit(solution)/shard_map/all_to_all | solution.py:502

commit v3 on v2

--- a/solution.py
+++ b/solution.py
@@ -55,7 +55,13 @@
     return jnp.sqrt(4.0 * jnp.pi / total)
 
 
-def project_kernel(orbitals, potentials, earlier, sums):
+def two_products(value, matrix):
+    high, low = split(value)
+    dot = functools.partial(jnp.dot, preferred_element_type=jnp.float32)
+    return dot(high, matrix) + dot(low, matrix)
+
+
+def project_kernel(orbitals, potentials, earlier, later, out, sums):
     count, planes, rows, width = orbitals.shape
     npot = potentials.shape[0]
     halves = width // LANES
@@ -83,13 +89,13 @@
 
     @pl.when(pl.program_id(0) == pl.num_programs(0) - 1)
     def _():
-        sums[:, 0, :] = jnp.sum(sums[...], axis=1)
-
-
-def project(orbitals, potentials, earlier):
+        out[...] = jnp.sum(sums[...], axis=1)
+
+
+def project(orbitals, potentials, earlier, later):
     count, planes, rows, width = orbitals.shape
     npot = potentials.shape[0]
-    step = 4
+    step = TILE
     total = (npot + 1) * count
     sums = pl.pallas_call(
         project_kernel,
@@ -98,15 +104,55 @@
             pl.BlockSpec((count, step, rows, width), lambda i: (0, i, 0, 0)),
             pl.BlockSpec((npot, step, rows, width), lambda i: (0, i, 0, 0)),
             pl.BlockSpec(memory_space=pl.ANY),
+            pl.BlockSpec(memory_space=pl.ANY),
         ],
-        out_specs=pl.BlockSpec((total, TILE, LANES), lambda i: (0, 0, 0)),
-        out_shape=jax.ShapeDtypeStruct((total, TILE, LANES), jnp.float32),
+        out_specs=pl.BlockSpec((total, LANES), lambda i: (0, 0)),
+        out_shape=jax.ShapeDtypeStruct((total, LANES), jnp.float32),
+        scratch_shapes=[pltpu.VMEM((total, TILE, LANES), jnp.float32)],
         compiler_params=pltpu.CompilerParams(vmem_limit_bytes=60 << 20),
-    )(orbitals, potentials, earlier)
-    return sums[:, 0, :]
-
-
-def edges_kernel(orbitals, potentials, local, first, last, tiles, sems):
+    )(orbitals, potentials, earlier, later)
+    return sums
+
+
+def reorder_kernel(*refs):
+    order, fields = refs[0], refs[1:]
+    sources, targets = fields[:len(fields) // 2], fields[len(fields) // 2:]
+    width = order.shape[0]
+    joined = jnp.concatenate([source[...].reshape(-1, width) for source in sources], axis=0)
+    value = two_products(joined, order[...])
+    at = 0
+    for target in targets:
+        size = target.size // width
+        part = value[at:at + size]
+        if target is targets[-1]:
+            part = 1.0 - 2.0 * part
+        target[...] = part.reshape(target.shape)
+        at += size
+
+
+def reorder(fields, order):
+    planes, _, width = fields[-1].shape
+    step = TILE
+
+    def spec(field):
+        lead = field.ndim - 3
+        shape = (*field.shape[:lead], step, *field.shape[lead + 1:])
+        return pl.BlockSpec(shape, lambda i: (0,) * lead + (i, 0, 0))
+
+    specs = [spec(field) for field in fields]
+    size = sum(field.size for field in fields)
+    return pl.pallas_call(
+        reorder_kernel,
+        grid=(planes // step,),
+        in_specs=[pl.BlockSpec((width, width), lambda i: (0, 0))] + specs,
+        out_specs=specs,
+        out_shape=[jax.ShapeDtypeStruct(v.shape, jnp.float32) for v in fields],
+        compiler_params=pltpu.CompilerParams(vmem_limit_bytes=60 << 20),
+        cost_estimate=pl.CostEstimate(flops=4 * size * width, bytes_accessed=8 * size, transcendentals=0),
+    )(order, *fields)
+
+
+def edges_kernel(orbitals, potentials, local, order, first, last, tiles, packed, sems):
     fields = []
     for source in (orbitals, potentials):
         fields += [source.at[i] for i in range(source.shape[0])]
@@ -122,38 +168,44 @@
             copies.append(copy)
     for copy in copies:
         copy.wait()
+    size = planes * HALO
     for side, (out, begin) in enumerate(((first, 0), (last, TILE - HALO))):
         for i in range(len(fields)):
             for z in range(planes):
-                out[i, z * HALO:(z + 1) * HALO, :] = tiles[side, i, z, begin:begin + HALO, :]
-
-
-def pack_edges(orbitals, potentials, local):
+                packed[i * size + z * HALO:i * size + (z + 1) * HALO, :] = tiles[side, i, z, begin:begin + HALO, :]
+        value = two_products(packed[...], order[...])
+        diagonal = size * (len(fields) - 1)
+        out[0:len(fields) - 1] = value[:diagonal].reshape(len(fields) - 1, size, width)
+        out[len(fields) - 1] = 1.0 - 2.0 * value[diagonal:]
+
+
+def pack_edges(orbitals, potentials, local, order):
     planes, _, width = local.shape
     fields = orbitals.shape[0] + potentials.shape[0] + 1
     vmem = pl.BlockSpec(memory_space=pltpu.VMEM)
     edge = jax.ShapeDtypeStruct((fields, planes * HALO, width), jnp.float32)
     return pl.pallas_call(
         edges_kernel,
-        in_specs=[pl.BlockSpec(memory_space=pl.ANY)] * 3,
+        in_specs=[pl.BlockSpec(memory_space=pl.ANY)] * 3 + [vmem],
         out_specs=[vmem] * 2,
         out_shape=[edge] * 2,
         scratch_shapes=[
             pltpu.VMEM((2, fields, planes, TILE, width), jnp.float32),
+            pltpu.VMEM((fields * planes * HALO, width), jnp.float32),
             pltpu.SemaphoreType.DMA((2, fields)),
         ],
         compiler_params=pltpu.CompilerParams(vmem_limit_bytes=60 << 20),
-    )(orbitals, potentials, local)
+    )(orbitals, potentials, local, order)
 
 
 def stencil_kernel(
     geometry,
-    coefficients, constants, place_index, z_tables, x_table,
-    orbitals, potentials, local, low, high,
-    mine, partner, far,
-    orb, pot, loc, src, one, two, density, spectrum, low_rows, high_rows, z_table, table_sem, sems,
+    coefficients, constants, place_index, z_tables, x_tables,
+    orbitals, potentials, local, low, high, *refs,
 ):
-    pots, count, start, rows, strip, group = geometry
+    outs = refs[geometry[-1]:-15]
+    (orb, pot, loc, src, one, two, density, spectrum, low_rows, high_rows, z_table, x_table, table_sem, x_sem, sems) = refs[-15:]
+    pots, count, start, rows, strip, group, _ = geometry
     npot = len(pots)
     planes = local.shape[0]
     width = local.shape[2]
@@ -208,6 +260,8 @@
     band = place_index[2]
     table_copy = pltpu.make_async_copy(z_tables.at[band], z_table, table_sem)
     table_copy.start()
+    x_copy = pltpu.make_async_copy(x_tables, x_table, x_sem)
+    x_copy.start()
 
     for field in (src, one, two):
         for p in range(npot):
@@ -227,12 +281,6 @@
 
     pieces("loc", 0, end_copy)
 
-    def weights(z, _):
-        for half in range(halves):
-            loc[half, z] = 1.0 - 2.0 * loc[half, z]
-        return 0
-
-    lax.fori_loop(0, planes, weights, 0)
     for p in range(npot):
         pieces("pot", p, end_copy)
 
@@ -241,13 +289,12 @@
         return [(r, min(most, size - r)) for r in range(0, size, most)]
 
     def sides(center):
-        lane = lax.broadcasted_iota(jnp.int32, center[0].shape, 1)
-        down = [pltpu.roll(c, 1, 1) for c in center]
-        up = [pltpu.roll(c, LANES - 1, 1) for c in center]
-        zero = jnp.zeros_like(center[0])
-        down = [jnp.where(lane == 0, before, now) for before, now in zip([zero] + down[:-1], down)]
-        up = [jnp.where(lane == LANES - 1, after, now) for after, now in zip(up[1:] + [zero], up)]
-        return [a + b for a, b in zip(down, up)]
+        even, odd = center
+        lane = lax.broadcasted_iota(jnp.int32, even.shape, 1)
+        zero = jnp.zeros_like(even)
+        down = jnp.where(lane == 0, zero, pltpu.roll(odd, 1, 1))
+        up = jnp.where(lane == LANES - 1, zero, pltpu.roll(even, LANES - 1, 1))
+        return [odd + down, even + up]
 
     def apply(field, offset, size, loc_offset, finish, step):
         z0 = step * group
@@ -332,52 +379,44 @@
     lax.fori_loop(0, count, orbital, 0)
 
     table_copy.wait()
+    x_copy.wait()
     z_parts = (z_table[0], z_table[1])
     x_parts = (x_table[0], x_table[1])
-    share = mine.shape[1] // npot
+    share = outs[0].shape[2]
     block = min(share, 2 * LANES)
-    for p in range(npot):
-        for tile in range(rows // TILE):
-            span = pl.ds(tile * TILE, TILE)
-            value = jnp.concatenate(
-                [density[h, p, :, span, :].reshape(planes * TILE, LANES) for h in range(halves)], axis=-1
-            )
-            value = product(z_parts, split(value), ((1,), (0,)))
-            spectrum[:, span, :] = value.reshape(planes, TILE, width)
-        for piece in range(planes * rows // block):
-            at = piece * block
-            value = spectrum[at // rows:(at + block) // rows].reshape(block, width)
-            value = product(x_parts, split(value), ((1,), (1,)))
-            for out, low_end, high_end in ((mine, 0, share), (partner, share, 2 * share)):
-                if low_end <= at < high_end:
-                    out[:, p * share + at - low_end:p * share + at - low_end + block] = value
-            if at >= 2 * share:
-                part, at = divmod(at - 2 * share, share)
-                column = (part * npot + p) * share + at
-                far[:, column:column + block] = value
-
-
-def stencil(pots, start, rows, group, coefficients, constants, edges, tables, fields, halos):
+    places = [(out, i) for out in outs for i in range(out.shape[0])]
+    for tile in range(rows // TILE):
+        span = pl.ds(tile * TILE, TILE)
+        value = jnp.concatenate(
+            [density[h, 0, :, span, :].reshape(planes * TILE, LANES) for h in range(halves)], axis=-1
+        )
+        value = product(z_parts, split(value), ((1,), (0,)))
+        spectrum[:, span, :] = value.reshape(planes, TILE, width)
+    for piece in range(planes * rows // block):
+        at = piece * block
+        value = spectrum[at // rows:(at + block) // rows].reshape(block, width)
+        value = product(x_parts, split(value), ((1,), (1,)))
+        out, i = places[at // share]
+        out[i, :, at % share:at % share + block] = value
+
+
+def stencil(pots, start, rows, group, coefficients, constants, edges, tables, fields, halos, blocks, earlier=()):
     orbitals, potentials, local = fields
     count, planes, strip, width = orbitals.shape
     halves = width // LANES
     npot = len(pots)
     padded = rows + 2 * TILE
-    share = planes * rows // 4
-    geometry = (pots, count, start, rows, strip, group)
+    share = planes * rows // sum(blocks)
+    geometry = (pots, count, start, rows, strip, group, len(earlier))
     vmem = pl.BlockSpec(memory_space=pltpu.VMEM)
     smem = pl.BlockSpec(memory_space=pltpu.SMEM)
     anywhere = pl.BlockSpec(memory_space=pl.ANY)
     f32 = jnp.float32
     return pl.pallas_call(
         functools.partial(stencil_kernel, geometry),
-        in_specs=[smem, smem, smem, anywhere, vmem] + [anywhere] * 5,
-        out_specs=[vmem] * 3,
-        out_shape=[
-            jax.ShapeDtypeStruct((width, npot * share), f32),
-            jax.ShapeDtypeStruct((width, npot * share), f32),
-            jax.ShapeDtypeStruct((width, npot * 2 * share), f32),
-        ],
+        in_specs=[smem, smem, smem, anywhere, anywhere] + [anywhere] * (5 + len(earlier)),
+        out_specs=[vmem] * len(blocks),
+        out_shape=[jax.ShapeDtypeStruct((i, width, share), f32) for i in blocks],
         scratch_shapes=[
             pltpu.VMEM((halves, count, planes, padded, LANES), f32),
             pltpu.VMEM((halves, npot, planes, padded, LANES), f32),
@@ -390,42 +429,57 @@
             pltpu.VMEM((halves, *halos[0].shape[:2], LANES), f32),
             pltpu.VMEM((halves, *halos[0].shape[:2], LANES), f32),
             pltpu.VMEM(tables[0].shape[1:], jnp.bfloat16),
+            pltpu.VMEM(tables[1].shape, jnp.bfloat16),
+            pltpu.SemaphoreType.DMA(()),
             pltpu.SemaphoreType.DMA(()),
             pltpu.SemaphoreType.DMA((1 + npot + count, halves, 3)),
         ],
-        compiler_params=pltpu.CompilerParams(vmem_limit_bytes=60 << 20),
+        compiler_params=pltpu.CompilerParams(vmem_limit_bytes=63 << 20),
         cost_estimate=pl.CostEstimate(flops=1 << 34, bytes_accessed=64 << 20, transcendentals=0),
-    )(coefficients, constants, edges, *tables, orbitals, potentials, local, *halos)
-
-
-def finish_kernel(received, table, weight, out):
-    parts, x_share, lanes = received.shape
-    z_share = out.shape[0]
-    strip = lanes // z_share
+    )(coefficients, constants, edges, *tables, orbitals, potentials, local, *halos, *earlier)
+
+
+def finish_kernel(pieces, received, table, weight, *refs):
+    out = refs[-1]
+    parts, x_share, _ = received.shape
+    z_share = out.shape[1]
+    strip = sum(pieces)
     table_parts = (table[0], table[1])
     lane = lax.broadcasted_iota(jnp.int32, (x_share, LANES), 1)
-    lower = lane < strip
-    for pair in range(z_share // 2):
-        columns = slice(pair * LANES, (pair + 1) * LANES)
-        blocks = [received[i, :, columns] for i in range(parts)]
-        rolled = [pltpu.roll(b, strip, 1) for b in blocks]
-        even = [jnp.where(lower, blocks[i], rolled[i + 1]) for i in range(0, parts, 2)]
-        odd = [jnp.where(lower, rolled[i], blocks[i + 1]) for i in range(0, parts, 2)]
-        both = jnp.concatenate([jnp.concatenate(even, axis=-1), jnp.concatenate(odd, axis=-1)], axis=0)
-        value = product(split(both), table_parts, ((1,), (0,)))
-        out[2 * pair] = value[:x_share] * weight[2 * pair]
-        out[2 * pair + 1] = value[x_share:] * weight[2 * pair + 1]
-
-
-def finish(received, table, weight):
-    vmem = pl.BlockSpec(memory_space=pltpu.VMEM)
+    joined = []
+    for k in range(z_share):
+        columns = []
+        for first in range(0, parts, LANES // strip):
+            value, target = None, 0
+            for source in range(first, first + LANES // strip):
+                base = 0
+                for rows in pieces:
+                    at = base + k * rows
+                    tile = received[source, :, at // LANES * LANES:at // LANES * LANES + LANES]
+                    turn = (target - at) % LANES
+                    tile = pltpu.roll(tile, turn, 1) if turn else tile
+                    value = tile if value is None else jnp.where(lane < target, value, tile)
+                    base += z_share * rows
+                    target += rows
+            columns.append(value)
+        joined.append(jnp.concatenate(columns, axis=-1))
+    value = product(split(jnp.concatenate(joined, axis=0)), table_parts, ((1,), (0,)))
+    for k in range(z_share):
+        out[0, k] = value[k * x_share:(k + 1) * x_share] * weight[k]
+
+
+def finish(p, npot, pieces, received, table, weight, result):
+    whole = [received, table, weight]
+    specs = [pl.BlockSpec(v.shape, lambda i, n=v.ndim: (0,) * n) for v in whole]
     return pl.pallas_call(
-        finish_kernel,
-        in_specs=[vmem] * 3,
-        out_specs=vmem,
-        out_shape=jax.ShapeDtypeStruct(weight.shape, jnp.float32),
+        functools.partial(finish_kernel, pieces),
+        grid=(1,),
+        in_specs=specs + ([] if result is None else [pl.BlockSpec(memory_space=pl.ANY)]),
+        out_specs=pl.BlockSpec((1, *weight.shape), lambda i: (p, 0, 0, 0)),
+        out_shape=jax.ShapeDtypeStruct((npot, *weight.shape), jnp.float32),
+        input_output_aliases={} if result is None else {3: 0},
         compiler_params=pltpu.CompilerParams(vmem_limit_bytes=40 << 20),
-    )(received, table, weight)
+    )(*whole, *([] if result is None else [result]))
 
 
 def total_over(values, axis):
@@ -446,12 +500,14 @@
     band, place = lax.axis_index("band"), lax.axis_index("gy")
     z_share, x_share = nz // bands, nx // gy
 
-    first, last = pack_edges(orbitals, potentials, local_potential)
+    along_x = np.concatenate([np.arange(0, nx, 2), np.arange(1, nx, 2)])
+    order = jnp.asarray(np.eye(nx)[:, along_x], jnp.bfloat16)
+    first, last = pack_edges(orbitals, potentials, local_potential, order)
     forward = [(i, i + 1) for i in range(gy - 1)]
     backward = [(b, a) for a, b in forward]
     halos = (lax.ppermute(last, "gy", forward), lax.ppermute(first, "gy", backward))
-    sums = total_over(project(orbitals, potentials, first), "gy")
-    fields = (orbitals, potentials, local_potential)
+    sums = total_over(project(orbitals, potentials, first, last), "gy")
+    fields = reorder((orbitals, potentials, local_potential), order)
     totals = jnp.sum(sums, axis=1).reshape(npot + 1, count)
     coefficients = (totals[:npot] / totals[npot]).reshape(-1)
 
@@ -461,52 +517,66 @@
     fourth = 1.0 + 8.0 * s * s * less_one
     unit = 2.0 * spread_half
     constants = jnp.stack([unit * s, unit * unit * less_one, -32.0 / (spread_half * unit**3) / fourth], axis=1)
-    edges = jnp.stack([(place == 0).astype(jnp.int32), (place == gy - 1).astype(jnp.int32), band])
+    place_index = jnp.stack([(place == 0).astype(jnp.int32), (place == gy - 1).astype(jnp.int32), band])
 
     sine_z = sine_values(nz)
     paired = bands == 4
-    if paired:
-        orders = [[b, b ^ 1] + ([2, 3] if b < 2 else [1, 0]) for b in range(bands)]
-    else:
-        orders = [list(range(bands))] * bands
-    by_band = []
-    for order in orders:
-        index = np.concatenate([np.arange(z_share) + z_share * o for o in order])
-        by_band.append(two_parts(np.kron(sine_z[index], np.eye(TILE))))
-    z_table = jnp.asarray(np.stack(by_band))
-    tables = (z_table, jnp.asarray(two_parts(sine_values(nx))))
+    plain = list(range(bands))
+    near_first = [[b, b ^ 1] + ([2, 3] if b < 2 else [1, 0]) for b in range(bands)] if paired else [plain] * bands
+
+    def z_tables(orders):
+        by_band = []
+        for order in orders:
+            index = np.concatenate([np.arange(z_share) + z_share * o for o in order])
+            by_band.append(two_parts(np.kron(sine_z[index], np.eye(TILE))))
+        return jnp.asarray(np.stack(by_band))
+
+    x_table = jnp.asarray(two_parts(sine_values(nx)[:, along_x]))
     z_index = band * z_share + jnp.arange(z_share, dtype=jnp.int32)
     x_index = place * x_share + jnp.arange(x_share, dtype=jnp.int32)
     weight = coulomb(z_index, x_index, jnp.arange(ny, dtype=jnp.int32), (nz, nx, ny))
 
     sine_y = sine_values(ny)
     y_table = jnp.asarray(two_parts(sine_y))
+    def exchange(total):
+        spread = total.reshape(gy, x_share, -1)
+        return lax.all_to_all(spread, "gy", split_axis=0, concat_axis=0, tiled=True)
+
+    def share_out(p, start, rows, blocks, earlier=()):
+        tables = (z_tables(near_first if paired else [plain] * bands), x_table)
+        return stencil(
+            (p,), start, rows, 16, coefficients, constants, place_index, tables, fields, halos, blocks, earlier
+        )
+
+    def inward(far):
+        sent = lax.ppermute(far, "band", [(0, 1), (3, 2)])
+        return far[:1] + sent[:1], far[1:] + sent[1:]
+
+    def outward(partner, close, distant):
+        return (
+            lax.ppermute(close, "band", [(1, 2), (2, 1)]),
+            lax.ppermute(distant, "band", [(1, 3), (2, 0)]),
+            lax.ppermute(partner, "band", [(0, 1), (1, 0), (2, 3), (3, 2)]),
+        )
+
+    def add_up(mine, got):
+        return (mine + got[2] + (got[0] + got[1]))[0]
+
+    if paired and 2 * strip == LANES:
+        result = None
+        for p in range(npot):
+            mine, partner, far = share_out(p, 0, strip, (1, 1, 2))
+            far = far + lax.ppermute(far, "band", [(0, 1), (3, 2)])
+            total = add_up(mine, outward(partner, far[:1], far[1:]))
+            result = finish(p, npot, (strip,), exchange(total), y_table, weight, result)
+        return result
     outs = []
     for p in range(npot):
-        mine, partner, far = stencil(
-            (p,), 0, strip, 16, coefficients, constants, edges, tables, fields, halos
-        )
-        share = mine.shape[1]
-        if paired:
-            inward = lax.ppermute(far, "band", [(0, 1), (3, 2)])
-            swapped = lax.ppermute(partner, "band", [(0, 1), (1, 0), (2, 3), (3, 2)])
-            close = far[:, :share] + inward[:, :share]
-            distant = far[:, share:] + inward[:, share:]
-            close = lax.ppermute(close, "band", [(1, 2), (2, 1)])
-            distant = lax.ppermute(distant, "band", [(1, 3), (2, 0)])
-            total = mine + swapped + (close + distant)
-        else:
-            joined = jnp.concatenate([mine, partner, far], axis=1)
-            total = lax.psum_scatter(joined, "band", scatter_dimension=1, tiled=True)
-        spread = total.reshape(gy, x_share, -1)
-        received = lax.all_to_all(spread, "gy", split_axis=0, concat_axis=0, tiled=True)
-        if paired and 2 * strip == LANES:
-            outs.append(finish(received, y_table, weight))
-        else:
-            terms = received.reshape(gy, x_share, z_share, strip)
-            table = jnp.asarray(sine_y, f32).reshape(gy, strip, ny)
-            value = jnp.einsum("sjky,sym->kjm", terms, table, precision=lax.Precision.HIGHEST)
-            outs.append(value * weight)
+        total = lax.psum_scatter(share_out(p, 0, strip, (bands,))[0], "band", scatter_dimension=0, tiled=True)
+        terms = exchange(total).reshape(gy, x_share, z_share, strip)
+        table = jnp.asarray(sine_y, f32).reshape(gy, strip, ny)
+        value = jnp.einsum("sjky,sym->kjm", terms, table, precision=lax.Precision.HIGHEST)
+        outs.append(value * weight)
     return jnp.stack(outs)
 
 

time: 156 us -> 154 us (0.987)
  starting transfers between devices: 41.9 us -> 34.3 us
  waiting for transfers between devices: 35.7 us -> 41.8 us
  other arithmetic: 11.5 us -> 8.9 us
  Pallas kernels: 63 us -> 64.6 us
    ppermute x8, waiting for transfers between devices: 18.4 us -> 31.5 us  [the longest x2 12.9 us: per_device(): far = far + lax.ppermute(far, 'band', [(0, 1), (3, 2)])]
    pallas_call x2 -> x3, Pallas kernels: 2.57 us -> 14.7 us  [the longest x1 11.9 us: reorder(): pl.pallas_call(reorder_kernel, grid=(planes // step,), in_specs=[pl.Block...]
    pallas_call x2, Pallas kernels: 49 us -> 38.5 us  [stencil(): pl.pallas_call(functools.partial(stencil_kernel, geometry), in_specs=[sme...]
    all_to_all x2, starting transfers between devices: 16.7 us -> 6.98 us  [exchange(): return lax.all_to_all(spread, 'gy', split_axis=0, concat_axis=0, tiled=True)]
    all_to_all x2, waiting for transfers between devices: 15.3 us -> 7.88 us  [exchange(): return lax.all_to_all(spread, 'gy', split_axis=0, concat_axis=0, tiled=True)]
  transfers between devices with their start and end apart: 15 -> 15, of which waited for: 7 -> 8; matrix products, arithmetic and copies ran while one was open for 7% -> 7% of each run, Pallas kernels for 22% -> 25%
where the time goes in v3:
time: 154 us; the launch traced here: 153 us
  Pallas kernels  64.6 us (42%)
  waiting for transfers between devices  41.8 us (27%)
  starting transfers between devices  34.3 us (22%)
  other arithmetic  8.9 us (6%)
  local copies, waits for them, and re-layouts  3.47 us (2%)
    pallas_call x2, Pallas kernels, stencil(): pl.pallas_call(functools.partial(stencil_kernel, geometry), in_specs=[sme...  38.5 us
    ppermute x2, waiting for transfers between devices, per_device(): far = far + lax.ppermute(far, 'band', [(0, 1), (3, 2)])  12.9 us
    pallas_call x1, Pallas kernels, reorder(): pl.pallas_call(reorder_kernel, grid=(planes // step,), in_specs=[pl.Block...  11.9 us
    ppermute x2, waiting for transfers between devices, outward(): lax.ppermute(partner, 'band', [(0, 1), (1, 0), (2, 3), (3, 2)])  11.2 us
    all_to_all x2, waiting for transfers between devices, exchange(): return lax.all_to_all(spread, 'gy', split_axis=0, concat_axis=0, tiled=True)  7.88 us
    ppermute x3, starting transfers between devices, total_over(): lax.ppermute(values, axis, [(i, i ^ step) for i in range(count)])  7.49 us
    ppermute x2, waiting for transfers between devices, outward(): lax.ppermute(distant, 'band', [(1, 3), (2, 0)])  7.35 us
    all_to_all x2, starting transfers between devices, exchange(): return lax.all_to_all(spread, 'gy', split_axis=0, concat_axis=0, tiled=True)  6.98 us
  transfers between devices with their start and end apart: 15, of which 8 were waited for; matrix products, arithmetic and copies ran while one was open for 7% of the time, Pallas kernels for 25%

profile of v3, /device:TPU:0, one launch (start us, length us, event | category | flops | bytes accessed | tf_op | source)
XLA Modules:
  0.0 153.3 jit_solution(12579945747831957374)
XLA Ops:
  0.0 5.0 %shard_map.91 = (f32[7,96,256]{2,1,0:T(8,128)}, f32[7,96,256]{2,1,0:T(8,128)}) custom-call(f32[4,32,64,256]{3,2,1,0:T(8,128)} %refs_1_.1, f32[2,32,64,256]{3,2,1,0:T(8,128)} %refs_2_.1, f32[32,64,256]{2,1,0:T(8,128)} %refs_3_.1, bf16[256,256]{1,0:T(8,128)(2,1)} %constant.63.clone.order.refs_0_), custom_call_target="tpu_custom_call" | custom-call | tf_op jit(solution)/shard_map/pallas_call | solution.py:187
  5.0 2.4 %collective-permute-start.3 = (f32[7,96,256]{2,1,0:T(8,128)}, f32[7,96,256]{2,1,0:T(8,128)S(1)}, u32[]{:S(2)}, u32[]{:S(2)}) collective-permute-start(f32[7,96,256]{2,1,0:T(8,128)} %get-tuple-element.17.later), channel_id=1, source_target_pairs={{0,1},{1,2},{2,3},{3,4},{4,5},{5,6},{6,7},{8,9},{9,10},{10,11},{11... | collective-permute-start | bytes 2064392 | tf_op jit(solution)/shard_map/ppermute | solution.py:508
  8.7 6.4 %shard_map.92 = f32[12,128]{1,0:T(8,128)} custom-call(f32[4,32,64,256]{3,2,1,0:T(8,128)} %refs_1_.1, f32[2,32,64,256]{3,2,1,0:T(8,128)} %refs_2_.1, f32[7,96,256]{2,1,0:T(8,128)} %get-tuple-element.16.earlier, f32[7,96,256]{2,1,0:T(8,128)} %get-tuple-element.17.later), custom_call_target="tpu_custom_call" | custom-call | tf_op jit(solution)/shard_map/pallas_call | solution.py:100
  15.1 3.2 %collective-permute-start = (f32[12,128]{1,0:T(8,128)}, f32[12,128]{1,0:T(8,128)S(1)}, u32[]{:S(2)}, u32[]{:S(2)}) collective-permute-start(f32[12,128]{1,0:T(8,128)} %shard_map.92), channel_id=1, source_target_pairs={{0,1},{1,0},{2,3},{3,2},{4,5},{5,4},{6,7},{7,6},{8,9},{9,8},{10,11... | collective-permute-start | bytes 18440 | tf_op jit(solution)/shard_map/ppermute | solution.py:489
  18.3 11.9 %shard_map.93 = (f32[4,32,64,256]{3,2,1,0:T(8,128)}, f32[2,32,64,256]{3,2,1,0:T(8,128)}, f32[32,64,256]{2,1,0:T(8,128)}) custom-call(bf16[256,256]{1,0:T(8,128)(2,1)} %constant.63.clone.order.refs_0_, f32[4,32,64,256]{3,2,1,0:T(8,128)} %refs_1_.1, f32[2,32,64,256]{3,2,1,0:T(8,128)} %refs_2_.1, f32[32,64,256]{2,1,0:T(8,128)} %refs_3_.1), custom_call_target="tpu_custom_call" | custom-call | flops 3758096384 | bytes 29360128 | tf_op jit(solution)/shard_map/pallas_call | solution.py:144
  30.5 1.7 %collective-permute-start.1 = (f32[12,128]{1,0:T(8,128)S(1)}, f32[12,128]{1,0:T(8,128)S(1)}, u32[]{:S(2)}, u32[]{:S(2)}) collective-permute-start(f32[12,128]{1,0:T(8,128)S(1)} %add.126), channel_id=1, source_target_pairs={{0,2},{1,3},{2,0},{3,1},{4,6},{5,7},{6,4},{7,5},{8,10},{9,11},{10,... | collective-permute-start | bytes 18440 | tf_op jit(solution)/shard_map/ppermute | solution.py:489
  34.2 2.6 %collective-permute-start.2 = (f32[12,128]{1,0:T(8,128)S(1)}, f32[12,128]{1,0:T(8,128)S(1)}, u32[]{:S(2)}, u32[]{:S(2)}) collective-permute-start(f32[12,128]{1,0:T(8,128)S(1)} %add.127), channel_id=1, source_target_pairs={{0,4},{1,5},{2,6},{3,7},{4,0},{5,1},{6,2},{7,3},{8,12},{9,13},{10,... | collective-permute-start | bytes 18440 | tf_op jit(solution)/shard_map/ppermute | solution.py:489
  40.2 19.2 %shard_map.95 = (f32[1,256,512]{2,1,0:T(8,128)}, f32[1,256,512]{2,1,0:T(8,128)}, f32[2,256,512]{2,1,0:T(8,128)}) custom-call(f32[8]{0:T(128)} %slice_divide_fusion.coefficients, f32[4,3]{1,0:T(4,128)} %pad_maximum_fusion.constants, s32[3]{0:T(128)} %pad_add_fusion.place_index, bf16[4,2,256,256]{3,2,1,0:T(8,128)(2,1)} %constant.66.clone.z_tables, ...), custom_call_target="tpu_custom_call" | custom-call | flops 17179869184 | bytes 67108864 | tf_op jit(solution)/shard_map/pallas_call | solution.py:415
  59.4 4.5 %collective-permute-start.10 = (f32[2,256,512]{2,1,0:T(8,128)}, f32[2,256,512]{2,1,0:T(8,128)}, u32[]{:S(2)}, u32[]{:S(2)}) collective-permute-start(f32[2,256,512]{2,1,0:T(8,128)} %get-tuple-element.26), channel_id=1, source_target_pairs={{0,8},{24,16},{1,9},{25,17},{2,10},{26,18},{3,11},{27,19},{4,12},{... | collective-permute-start | bytes 3145736 | tf_op jit(solution)/shard_map/ppermute | solution.py:569
  63.9 19.2 %shard_map.94 = (f32[1,256,512]{2,1,0:T(8,128)}, f32[1,256,512]{2,1,0:T(8,128)}, f32[2,256,512]{2,1,0:T(8,128)}) custom-call(f32[8]{0:T(128)} %slice_divide_fusion.coefficients, f32[4,3]{1,0:T(4,128)} %pad_maximum_fusion.constants, s32[3]{0:T(128)} %pad_add_fusion.place_index, bf16[4,2,256,256]{3,2,1,0:T(8,128)(2,1)} %constant.66.clone.z_tables, ...), custom_call_target="tpu_custom_call" | custom-call | flops 17179869184 | bytes 67108864 | tf_op jit(solution)/shard_map/pallas_call | solution.py:415
  83.1 1.5 collective-permute-start.6
  85.0 1.7 %add.154 = f32[2,256,512]{2,1,0:T(8,128)S(1)} add(f32[2,256,512]{2,1,0:T(8,128)} %get-tuple-element.26, f32[2,256,512]{2,1,0:T(8,128)} %collective-permute-done.10) | non-fusion elementwise | flops 262144 | bytes 3145728 | tf_op jit(solution)/shard_map/add | solution.py:569
  87.8 1.4 collective-permute-start.11
  90.6 5.3 %collective-permute-start.5 = (f32[1,256,512]{2,1,0:T(8,128)}, f32[1,256,512]{2,1,0:T(8,128)}, u32[]{:S(2)}, u32[]{:S(2)}) collective-permute-start(f32[1,256,512]{2,1,0:T(8,128)} %get-tuple-element.22), channel_id=1, source_target_pairs={{0,8},{8,0},{16,24},{24,16},{1,9},{9,1},{17,25},{25,17},{2,10},{10... | collective-permute-start | bytes 1572872 | tf_op jit(solution)/shard_map/ppermute | solution.py:559
  95.9 12.6 %collective-permute-done.6 = f32[2,256,512]{2,1,0:T(8,128)S(1)} collective-permute-done((f32[2,256,512]{2,1,0:T(8,128)}, f32[2,256,512]{2,1,0:T(8,128)S(1)}, u32[]{:S(2)}, u32[]{:S(2)}) %collective-permute-start.6) | collective-permute-done | bytes 1048608 | tf_op jit(solution)/shard_map/ppermute | solution.py:569
  110.6 9.1 %collective-permute-done.9 = f32[1,256,512]{2,1,0:T(8,128)} collective-permute-done((f32[1,256,512]{2,1,0:T(8,128)}, f32[1,256,512]{2,1,0:T(8,128)}, u32[]{:S(2)}, u32[]{:S(2)}) %collective-permute-start.9) | collective-permute-done | bytes 524320 | tf_op jit(solution)/shard_map/ppermute | solution.py:559
  121.1 2.4 %add_add_fusion = f32[1,256,512]{2,1,0:T(8,128)} fusion(f32[1,256,512]{2,1,0:T(8,128)} %collective-permute-done.11, f32[1,256,512]{2,1,0:T(8,128)} %collective-permute-done.12, f32[1,256,512]{2,1,0:T(8,128)S(1)} %copy-done.3, f32[1,256,512]{2,1,0:T(8,128)} %collective-permute-done.9), kind=kLoop, calls=%fused_computation | loop fusion | flops 393216 | bytes 2621440 | tf_op jit(solution)/shard_map/add | solution.py:563
  123.5 3.5 %all-to-all-start.1 = ((f32[8,32,512]{2,1,0:T(8,128)}), f32[8,32,512]{2,1,0:T(8,128)S(1)}, u32[]{:S(2)}, u32[]{:S(2)}) async-start(f32[8,32,512]{2,1,0:T(8,128)} %bitcast.7), calls=%async_computation.1 | async-start | bytes 1048576 | tf_op jit(solution)/shard_map/all_to_all | solution.py:543
  127.0 2.1 %collective-permute-done.5 = f32[1,256,512]{2,1,0:T(8,128)} collective-permute-done((f32[1,256,512]{2,1,0:T(8,128)}, f32[1,256,512]{2,1,0:T(8,128)}, u32[]{:S(2)}, u32[]{:S(2)}) %collective-permute-start.5) | collective-permute-done | bytes 524320 | tf_op jit(solution)/shard_map/ppermute | solution.py:559
  129.1 7.3 %collective-permute-done.8 = f32[1,256,512]{2,1,0:T(8,128)} collective-permute-done((f32[1,256,512]{2,1,0:T(8,128)}, f32[1,256,512]{2,1,0:T(8,128)}, u32[]{:S(2)}, u32[]{:S(2)}) %collective-permute-start.8) | collective-permute-done | bytes 524320 | tf_op jit(solution)/shard_map/ppermute | solution.py:558
  136.4 2.2 %add_add_fusion.1 = f32[1,256,512]{2,1,0:T(8,128)} fusion(f32[1,256,512]{2,1,0:T(8,128)S(1)} %collective-permute-done.7, f32[1,256,512]{2,1,0:T(8,128)} %collective-permute-done.8, f32[1,256,512]{2,1,0:T(8,128)S(1)} %copy-done.2, f32[1,256,512]{2,1,0:T(8,128)} %collective-permute-done.5), kind=kLoop, calls=%fused_computation.2 | loop fusion | flops 393216 | bytes 2621440 | tf_op jit(solution)/shard_map/add | solution.py:563
  138.7 3.5 %all-to-all-start = ((f32[8,32,512]{2,1,0:T(8,128)}), f32[8,32,512]{2,1,0:T(8,128)S(1)}, u32[]{:S(2)}, u32[]{:S(2)}) async-start(f32[8,32,512]{2,1,0:T(8,128)} %bitcast.6), calls=%async_computation | async-start | bytes 1048576 | tf_op jit(solution)/shard_map/all_to_all | solution.py:543
  142.6 1.4 shard_map.96.refs_0_
  144.0 7.9 %all-to-all-done.received = f32[8,32,512]{2,1,0:T(8,128)S(1)} async-done(((f32[8,32,512]{2,1,0:T(8,128)}), f32[8,32,512]{2,1,0:T(8,128)S(1)}, u32[]{:S(2)}, u32[]{:S(2)}) %all-to-all-start) | async-done | bytes 524320 | tf_op jit(solution)/shard_map/all_to_all | solution.py:543
  (51 shorter events, 14.8 us)
Async XLA Ops:
  5.0 34.3 %collective-permute-start.3 = (f32[7,96,256]{2,1,0:T(8,128)}, f32[7,96,256]{2,1,0:T(8,128)S(1)}, u32[]{:S(2)}, u32[]{:S(2)}) collective-permute-start(f32[7,96,256]{2,1,0:T(8,128)} %get-tuple-element.17.later), channel_id=1, source_target_pairs={{0,1},{1,2},{2,3},{3,4},{4,5},{5,6},{6,7},{8,9},{9,10},{10,11},{11... | collective-permute-start | bytes 2064392 | tf_op jit(solution)/shard_map/ppermute | solution.py:508
  7.4 31.9 %collective-permute-start.4 = (f32[7,96,256]{2,1,0:T(8,128)}, f32[7,96,256]{2,1,0:T(8,128)}, u32[]{:S(2)}, u32[]{:S(2)}) collective-permute-start(f32[7,96,256]{2,1,0:T(8,128)} %get-tuple-element.16.earlier), channel_id=1, source_target_pairs={{1,0},{2,1},{3,2},{4,3},{5,4},{6,5},{7,6},{9,8},{10,9},{11,10},{12... | collective-permute-start | bytes 2064392 | tf_op jit(solution)/shard_map/ppermute | solution.py:508
  15.1 15.1 %copy-start.5 = (f32[4]{0:T(128)S(1)}, f32[4]{0:T(128)}, u32[]{:S(2)}) copy-start(f32[4]{0:T(128)} %param.12) | copy-start | bytes 52
  15.1 15.4 %copy-start.4 = (f32[12,128]{1,0:T(8,128)S(1)}, f32[12,128]{1,0:T(8,128)}, u32[]{:S(2)}) copy-start(f32[12,128]{1,0:T(8,128)} %shard_map.92) | copy-start | bytes 18436
  15.1 15.4 %collective-permute-start = (f32[12,128]{1,0:T(8,128)}, f32[12,128]{1,0:T(8,128)S(1)}, u32[]{:S(2)}, u32[]{:S(2)}) collective-permute-start(f32[12,128]{1,0:T(8,128)} %shard_map.92), channel_id=1, source_target_pairs={{0,1},{1,0},{2,3},{3,2},{4,5},{5,4},{6,7},{7,6},{8,9},{9,8},{10,11... | collective-permute-start | bytes 18440 | tf_op jit(solution)/shard_map/ppermute | solution.py:489
  30.5 3.7 %collective-permute-start.1 = (f32[12,128]{1,0:T(8,128)S(1)}, f32[12,128]{1,0:T(8,128)S(1)}, u32[]{:S(2)}, u32[]{:S(2)}) collective-permute-start(f32[12,128]{1,0:T(8,128)S(1)} %add.126), channel_id=1, source_target_pairs={{0,2},{1,3},{2,0},{3,1},{4,6},{5,7},{6,4},{7,5},{8,10},{9,11},{10,... | collective-permute-start | bytes 18440 | tf_op jit(solution)/shard_map/ppermute | solution.py:489
  34.2 4.2 %collective-permute-start.2 = (f32[12,128]{1,0:T(8,128)S(1)}, f32[12,128]{1,0:T(8,128)S(1)}, u32[]{:S(2)}, u32[]{:S(2)}) collective-permute-start(f32[12,128]{1,0:T(8,128)S(1)} %add.127), channel_id=1, source_target_pairs={{0,4},{1,5},{2,6},{3,7},{4,0},{5,1},{6,2},{7,3},{8,12},{9,13},{10,... | collective-permute-start | bytes 18440 | tf_op jit(solution)/shard_map/ppermute | solution.py:489
  39.3 0.9 copy-start.6
  59.4 25.6 %collective-permute-start.10 = (f32[2,256,512]{2,1,0:T(8,128)}, f32[2,256,512]{2,1,0:T(8,128)}, u32[]{:S(2)}, u32[]{:S(2)}) collective-permute-start(f32[2,256,512]{2,1,0:T(8,128)} %get-tuple-element.26), channel_id=1, source_target_pairs={{0,8},{24,16},{1,9},{25,17},{2,10},{26,18},{3,11},{27,19},{4,12},{... | collective-permute-start | bytes 3145736 | tf_op jit(solution)/shard_map/ppermute | solution.py:569
  83.1 25.4 %copy-start.1 = (f32[2,256,512]{2,1,0:T(8,128)S(1)}, f32[2,256,512]{2,1,0:T(8,128)}, u32[]{:S(2)}) copy-start(f32[2,256,512]{2,1,0:T(8,128)} %get-tuple-element.23) | copy-start | bytes 3145732
  83.1 25.3 %collective-permute-start.6 = (f32[2,256,512]{2,1,0:T(8,128)}, f32[2,256,512]{2,1,0:T(8,128)S(1)}, u32[]{:S(2)}, u32[]{:S(2)}) collective-permute-start(f32[2,256,512]{2,1,0:T(8,128)} %get-tuple-element.23), channel_id=1, source_target_pairs={{0,8},{24,16},{1,9},{25,17},{2,10},{26,18},{3,11},{27,19},{4,12},{... | collective-permute-start | bytes 3145736 | tf_op jit(solution)/shard_map/ppermute | solution.py:569
  84.6 35.1 %collective-permute-start.9 = (f32[1,256,512]{2,1,0:T(8,128)}, f32[1,256,512]{2,1,0:T(8,128)}, u32[]{:S(2)}, u32[]{:S(2)}) collective-permute-start(f32[1,256,512]{2,1,0:T(8,128)} %get-tuple-element.25), channel_id=1, source_target_pairs={{0,8},{8,0},{16,24},{24,16},{1,9},{9,1},{17,25},{25,17},{2,10},{10... | collective-permute-start | bytes 1572872 | tf_op jit(solution)/shard_map/ppermute | solution.py:559
  86.8 34.3 %copy-start.3 = (f32[1,256,512]{2,1,0:T(8,128)S(1)}, f32[1,256,512]{2,1,0:T(8,128)}, u32[]{:S(2)}) copy-start(f32[1,256,512]{2,1,0:T(8,128)} %get-tuple-element.24) | copy-start | bytes 1572868
  87.8 33.2 %collective-permute-start.11 = (f32[1,256,512]{2,1,0:T(8,128)}, f32[1,256,512]{2,1,0:T(8,128)}, u32[]{:S(2)}, u32[]{:S(2)}) collective-permute-start(f32[1,256,512]{2,1,0:T(8,128)} %get-tuple-element.28), channel_id=1, source_target_pairs={{8,16},{16,8},{9,17},{17,9},{10,18},{18,10},{11,19},{19,11},{12,20... | collective-permute-start | bytes 1572872 | tf_op jit(solution)/shard_map/ppermute | solution.py:557
  89.3 31.8 %collective-permute-start.12 = (f32[1,256,512]{2,1,0:T(8,128)}, f32[1,256,512]{2,1,0:T(8,128)}, u32[]{:S(2)}, u32[]{:S(2)}) collective-permute-start(f32[1,256,512]{2,1,0:T(8,128)} %get-tuple-element.27), channel_id=1, source_target_pairs={{8,24},{16,0},{9,25},{17,1},{10,26},{18,2},{11,27},{19,3},{12,28},... | collective-permute-start | bytes 1572872 | tf_op jit(solution)/shard_map/ppermute | solution.py:558
  90.6 45.9 %copy-start.2 = (f32[1,256,512]{2,1,0:T(8,128)S(1)}, f32[1,256,512]{2,1,0:T(8,128)}, u32[]{:S(2)}) copy-start(f32[1,256,512]{2,1,0:T(8,128)} %get-tuple-element.21) | copy-start | bytes 1572868
  90.6 38.5 %collective-permute-start.5 = (f32[1,256,512]{2,1,0:T(8,128)}, f32[1,256,512]{2,1,0:T(8,128)}, u32[]{:S(2)}, u32[]{:S(2)}) collective-permute-start(f32[1,256,512]{2,1,0:T(8,128)} %get-tuple-element.22), channel_id=1, source_target_pairs={{0,8},{8,0},{16,24},{24,16},{1,9},{9,1},{17,25},{25,17},{2,10},{10... | collective-permute-start | bytes 1572872 | tf_op jit(solution)/shard_map/ppermute | solution.py:559
  109.8 32.8 %copy-start = (bf16[2,512,512]{2,1,0:T(8,128)(2,1)S(1)}, bf16[2,512,512]{2,1,0:T(8,128)(2,1)}, u32[]{:S(2)}) copy-start(bf16[2,512,512]{2,1,0:T(8,128)(2,1)} %constant.65.clone.table) | copy-start | bytes 3145732
  109.8 19.3 %collective-permute-start.7 = (f32[1,256,512]{2,1,0:T(8,128)}, f32[1,256,512]{2,1,0:T(8,128)S(1)}, u32[]{:S(2)}, u32[]{:S(2)}) collective-permute-start(f32[1,256,512]{2,1,0:T(8,128)} %get-tuple-element.30), channel_id=1, source_target_pairs={{8,16},{16,8},{9,17},{17,9},{10,18},{18,10},{11,19},{19,11},{12,20... | collective-permute-start | bytes 1572872 | tf_op jit(solution)/shard_map/ppermute | solution.py:557
  119.7 16.7 %collective-permute-start.8 = (f32[1,256,512]{2,1,0:T(8,128)}, f32[1,256,512]{2,1,0:T(8,128)}, u32[]{:S(2)}, u32[]{:S(2)}) collective-permute-start(f32[1,256,512]{2,1,0:T(8,128)} %get-tuple-element.29), channel_id=1, source_target_pairs={{8,24},{16,0},{9,25},{17,1},{10,26},{18,2},{11,27},{19,3},{12,28},... | collective-permute-start | bytes 1572872 | tf_op jit(solution)/shard_map/ppermute | solution.py:558
  123.5 15.2 %all-to-all-start.1 = ((f32[8,32,512]{2,1,0:T(8,128)}), f32[8,32,512]{2,1,0:T(8,128)S(1)}, u32[]{:S(2)}, u32[]{:S(2)}) async-start(f32[8,32,512]{2,1,0:T(8,128)} %bitcast.7), calls=%async_computation.1 | async-start | bytes 1048576 | tf_op jit(solution)/shard_map/all_to_all | solution.py:543
  138.7 13.2 %all-to-all-start = ((f32[8,32,512]{2,1,0:T(8,128)}), f32[8,32,512]{2,1,0:T(8,128)S(1)}, u32[]{:S(2)}, u32[]{:S(2)}) async-start(f32[8,32,512]{2,1,0:T(8,128)} %bitcast.6), calls=%async_computation | async-start | bytes 1048576 | tf_op jit(solution)/shard_map/all_to_all | solution.py:543

commit v4 on v3

--- a/solution.py
+++ b/solution.py
@@ -61,7 +61,8 @@
     return dot(high, matrix) + dot(low, matrix)
 
 
-def project_kernel(orbitals, potentials, earlier, later, out, sums):
+def prepare_kernel(orbitals, potentials, local, order, earlier, later, out, *refs):
+    targets, sums = refs[:-1], refs[-1]
     count, planes, rows, width = orbitals.shape
     npot = potentials.shape[0]
     halves = width // LANES
@@ -69,6 +70,17 @@
     @pl.when(pl.program_id(0) == 0)
     def _():
         sums[...] = jnp.zeros_like(sums)
+
+    joined = jnp.concatenate([f[...].reshape(-1, width) for f in (orbitals, potentials, local)], axis=0)
+    value = two_products(joined, order[...])
+    at = 0
+    for target in targets:
+        size = target.size // width
+        part = value[at:at + size]
+        if target is targets[-1]:
+            part = 1.0 - 2.0 * part
+        target[...] = part.reshape(target.shape)
+        at += size
 
     def fold(value):
         return jnp.sum(value.reshape(rows // TILE, TILE, LANES), axis=0)
@@ -92,47 +104,11 @@
         out[...] = jnp.sum(sums[...], axis=1)
 
 
-def project(orbitals, potentials, earlier, later):
-    count, planes, rows, width = orbitals.shape
-    npot = potentials.shape[0]
+def prepare(fields, order, earlier, later):
+    orbitals, potentials, local = fields
+    planes, _, width = local.shape
     step = TILE
-    total = (npot + 1) * count
-    sums = pl.pallas_call(
-        project_kernel,
-        grid=(planes // step,),
-        in_specs=[
-            pl.BlockSpec((count, step, rows, width), lambda i: (0, i, 0, 0)),
-            pl.BlockSpec((npot, step, rows, width), lambda i: (0, i, 0, 0)),
-            pl.BlockSpec(memory_space=pl.ANY),
-            pl.BlockSpec(memory_space=pl.ANY),
-        ],
-        out_specs=pl.BlockSpec((total, LANES), lambda i: (0, 0)),
-        out_shape=jax.ShapeDtypeStruct((total, LANES), jnp.float32),
-        scratch_shapes=[pltpu.VMEM((total, TILE, LANES), jnp.float32)],
-        compiler_params=pltpu.CompilerParams(vmem_limit_bytes=60 << 20),
-    )(orbitals, potentials, earlier, later)
-    return sums
-
-
-def reorder_kernel(*refs):
-    order, fields = refs[0], refs[1:]
-    sources, targets = fields[:len(fields) // 2], fields[len(fields) // 2:]
-    width = order.shape[0]
-    joined = jnp.concatenate([source[...].reshape(-1, width) for source in sources], axis=0)
-    value = two_products(joined, order[...])
-    at = 0
-    for target in targets:
-        size = target.size // width
-        part = value[at:at + size]
-        if target is targets[-1]:
-            part = 1.0 - 2.0 * part
-        target[...] = part.reshape(target.shape)
-        at += size
-
-
-def reorder(fields, order):
-    planes, _, width = fields[-1].shape
-    step = TILE
+    total = (potentials.shape[0] + 1) * orbitals.shape[0]
 
     def spec(field):
         lead = field.ndim - 3
@@ -140,16 +116,18 @@
         return pl.BlockSpec(shape, lambda i: (0,) * lead + (i, 0, 0))
 
     specs = [spec(field) for field in fields]
-    size = sum(field.size for field in fields)
-    return pl.pallas_call(
-        reorder_kernel,
+    anywhere = pl.BlockSpec(memory_space=pl.ANY)
+    sums, *ordered = pl.pallas_call(
+        prepare_kernel,
         grid=(planes // step,),
-        in_specs=[pl.BlockSpec((width, width), lambda i: (0, 0))] + specs,
-        out_specs=specs,
-        out_shape=[jax.ShapeDtypeStruct(v.shape, jnp.float32) for v in fields],
+        in_specs=specs + [pl.BlockSpec((width, width), lambda i: (0, 0)), anywhere, anywhere],
+        out_specs=[pl.BlockSpec((total, LANES), lambda i: (0, 0))] + specs,
+        out_shape=[jax.ShapeDtypeStruct((total, LANES), jnp.float32)]
+        + [jax.ShapeDtypeStruct(f.shape, jnp.float32) for f in fields],
+        scratch_shapes=[pltpu.VMEM((total, TILE, LANES), jnp.float32)],
         compiler_params=pltpu.CompilerParams(vmem_limit_bytes=60 << 20),
-        cost_estimate=pl.CostEstimate(flops=4 * size * width, bytes_accessed=8 * size, transcendentals=0),
-    )(order, *fields)
+    )(*fields, order, earlier, later)
+    return sums, ordered
 
 
 def edges_kernel(orbitals, potentials, local, order, first, last, tiles, packed, sems):
@@ -506,8 +484,8 @@
     forward = [(i, i + 1) for i in range(gy - 1)]
     backward = [(b, a) for a, b in forward]
     halos = (lax.ppermute(last, "gy", forward), lax.ppermute(first, "gy", backward))
-    sums = total_over(project(orbitals, potentials, first, last), "gy")
-    fields = reorder((orbitals, potentials, local_potential), order)
+    sums, fields = prepare((orbitals, potentials, local_potential), order, first, last)
+    sums = total_over(sums, "gy")
     totals = jnp.sum(sums, axis=1).reshape(npot + 1, count)
     coefficients = (totals[:npot] / totals[npot]).reshape(-1)
 
@@ -545,7 +523,7 @@
     def share_out(p, start, rows, blocks, earlier=()):
         tables = (z_tables(near_first if paired else [plain] * bands), x_table)
         return stencil(
-            (p,), start, rows, 16, coefficients, constants, place_index, tables, fields, halos, blocks, earlier
+            (p,), start, rows, 32, coefficients, constants, place_index, tables, fields, halos, blocks, earlier
         )
 
     def inward(far):

time: 154 us -> 149 us (0.968)
  Pallas kernels: 64.6 us -> 58.4 us
    pallas_call x2 -> x1, Pallas kernels: 18.3 us -> 13.4 us  [prepare(): pl.pallas_call(prepare_kernel, grid=(planes // step,), in_specs=specs + [...]
  transfers between devices with their start and end apart: 15 -> 15, of which waited for: 8 -> 9; matrix products, arithmetic and copies ran while one was open for 7% -> 8% of each run, Pallas kernels for 25% -> 22%
where the time goes in v4:
time: 149 us
  Pallas kernels  58.4 us (39%)
  waiting for transfers between devices  41.9 us (28%)
  starting transfers between devices  35.1 us (24%)
  other arithmetic  9.55 us (6%)
  local copies, waits for them, and re-layouts  3.47 us (2%)
    pallas_call x2, Pallas kernels, stencil(): pl.pallas_call(functools.partial(stencil_kernel, geometry), in_specs=[sme...  37.2 us
    pallas_call x1, Pallas kernels, prepare(): pl.pallas_call(prepare_kernel, grid=(planes // step,), in_specs=specs + [...  13.4 us
    ppermute x2, waiting for transfers between devices, per_device(): far = far + lax.ppermute(far, 'band', [(0, 1), (3, 2)])  12.7 us
    ppermute x2, waiting for transfers between devices, outward(): lax.ppermute(partner, 'band', [(0, 1), (1, 0), (2, 3), (3, 2)])  11.6 us
    ppermute x3, starting transfers between devices, total_over(): lax.ppermute(values, axis, [(i, i ^ step) for i in range(count)])  8.05 us
    all_to_all x2, waiting for transfers between devices, exchange(): return lax.all_to_all(spread, 'gy', split_axis=0, concat_axis=0, tiled=True)  7.88 us
    all_to_all x2, starting transfers between devices, exchange(): return lax.all_to_all(spread, 'gy', split_axis=0, concat_axis=0, tiled=True)  6.98 us
    ppermute x2, waiting for transfers between devices, outward(): lax.ppermute(distant, 'band', [(1, 3), (2, 0)])  6.88 us
  transfers between devices with their start and end apart: 15, of which 9 were waited for; matrix products, arithmetic and copies ran while one was open for 8% of the time, Pallas kernels for 22%

profile of v4, /device:TPU:0, one launch (start us, length us, event | category | flops | bytes accessed | tf_op | source)
XLA Modules:
  0.0 148.6 jit_solution(11709783620588942122)
XLA Ops:
  0.0 5.0 %shard_map.91 = (f32[7,96,256]{2,1,0:T(8,128)}, f32[7,96,256]{2,1,0:T(8,128)}) custom-call(f32[4,32,64,256]{3,2,1,0:T(8,128)} %orbitals.3, f32[2,32,64,256]{3,2,1,0:T(8,128)} %potentials.3, f32[32,64,256]{2,1,0:T(8,128)} %local.3, bf16[256,256]{1,0:T(8,128)(2,1)} %constant.63.clone.order), custom_call_target="tpu_custom_call" | custom-call | tf_op jit(solution)/shard_map/pallas_call | solution.py:165
  5.0 2.4 %collective-permute-start.3 = (f32[7,96,256]{2,1,0:T(8,128)}, f32[7,96,256]{2,1,0:T(8,128)S(1)}, u32[]{:S(2)}, u32[]{:S(2)}) collective-permute-start(f32[7,96,256]{2,1,0:T(8,128)} %get-tuple-element.18.later), channel_id=1, source_target_pairs={{0,1},{1,2},{2,3},{3,4},{4,5},{5,6},{6,7},{8,9},{9,10},{10,11},{11... | collective-permute-start | bytes 2064392 | tf_op jit(solution)/shard_map/ppermute | solution.py:486
  8.7 13.4 %shard_map.92 = (f32[12,128]{1,0:T(8,128)}, f32[4,32,64,256]{3,2,1,0:T(8,128)}, f32[2,32,64,256]{3,2,1,0:T(8,128)}, f32[32,64,256]{2,1,0:T(8,128)}) custom-call(f32[4,32,64,256]{3,2,1,0:T(8,128)} %orbitals.3, f32[2,32,64,256]{3,2,1,0:T(8,128)} %potentials.3, f32[32,64,256]{2,1,0:T(8,128)} %local.3, bf16[256,256]{1,0:T(8,128)(2,1)} %constant.63.clone.order, ...), custom_call_target="tpu_custom_call" | custom-call | tf_op jit(solution)/shard_map/pallas_call | solution.py:120
  22.1 3.2 %collective-permute-start = (f32[12,128]{1,0:T(8,128)}, f32[12,128]{1,0:T(8,128)S(1)}, u32[]{:S(2)}, u32[]{:S(2)}) collective-permute-start(f32[12,128]{1,0:T(8,128)} %get-tuple-element.19), channel_id=1, source_target_pairs={{0,1},{1,0},{2,3},{3,2},{4,5},{5,4},{6,7},{7,6},{8,9},{9,8},{10,11... | collective-permute-start | bytes 18440 | tf_op jit(solution)/shard_map/ppermute | solution.py:467
  27.0 2.0 %collective-permute-start.1 = (f32[12,128]{1,0:T(8,128)S(1)}, f32[12,128]{1,0:T(8,128)S(1)}, u32[]{:S(2)}, u32[]{:S(2)}) collective-permute-start(f32[12,128]{1,0:T(8,128)S(1)} %add.126), channel_id=1, source_target_pairs={{0,2},{1,3},{2,0},{3,1},{4,6},{5,7},{6,4},{7,5},{8,10},{9,11},{10,... | collective-permute-start | bytes 18440 | tf_op jit(solution)/shard_map/ppermute | solution.py:467
  30.7 2.9 %collective-permute-start.2 = (f32[12,128]{1,0:T(8,128)S(1)}, f32[12,128]{1,0:T(8,128)S(1)}, u32[]{:S(2)}, u32[]{:S(2)}) collective-permute-start(f32[12,128]{1,0:T(8,128)S(1)} %add.127), channel_id=1, source_target_pairs={{0,4},{1,5},{2,6},{3,7},{4,0},{5,1},{6,2},{7,3},{8,12},{9,13},{10,... | collective-permute-start | bytes 18440 | tf_op jit(solution)/shard_map/ppermute | solution.py:467
  36.9 18.6 %shard_map.94 = (f32[1,256,512]{2,1,0:T(8,128)}, f32[1,256,512]{2,1,0:T(8,128)}, f32[2,256,512]{2,1,0:T(8,128)}) custom-call(f32[8]{0:T(128)} %slice_divide_fusion.coefficients, f32[4,3]{1,0:T(4,128)} %pad_maximum_fusion.constants, s32[3]{0:T(128)} %pad_add_fusion.place_index, bf16[4,2,256,256]{3,2,1,0:T(8,128)(2,1)} %constant.66.clone.z_tables, ...), custom_call_target="tpu_custom_call" | custom-call | flops 17179869184 | bytes 67108864 | tf_op jit(solution)/shard_map/pallas_call | solution.py:393
  55.5 4.5 %collective-permute-start.10 = (f32[2,256,512]{2,1,0:T(8,128)}, f32[2,256,512]{2,1,0:T(8,128)}, u32[]{:S(2)}, u32[]{:S(2)}) collective-permute-start(f32[2,256,512]{2,1,0:T(8,128)} %get-tuple-element.28), channel_id=1, source_target_pairs={{0,8},{24,16},{1,9},{25,17},{2,10},{26,18},{3,11},{27,19},{4,12},{... | collective-permute-start | bytes 3145736 | tf_op jit(solution)/shard_map/ppermute | solution.py:547
  60.0 18.6 %shard_map.93 = (f32[1,256,512]{2,1,0:T(8,128)}, f32[1,256,512]{2,1,0:T(8,128)}, f32[2,256,512]{2,1,0:T(8,128)}) custom-call(f32[8]{0:T(128)} %slice_divide_fusion.coefficients, f32[4,3]{1,0:T(4,128)} %pad_maximum_fusion.constants, s32[3]{0:T(128)} %pad_add_fusion.place_index, bf16[4,2,256,256]{3,2,1,0:T(8,128)(2,1)} %constant.66.clone.z_tables, ...), custom_call_target="tpu_custom_call" | custom-call | flops 17179869184 | bytes 67108864 | tf_op jit(solution)/shard_map/pallas_call | solution.py:393
  78.6 1.7 %collective-permute-start.6 = (f32[2,256,512]{2,1,0:T(8,128)}, f32[2,256,512]{2,1,0:T(8,128)S(1)}, u32[]{:S(2)}, u32[]{:S(2)}) collective-permute-start(f32[2,256,512]{2,1,0:T(8,128)} %get-tuple-element.25), channel_id=1, source_target_pairs={{0,8},{24,16},{1,9},{25,17},{2,10},{26,18},{3,11},{27,19},{4,12},{... | collective-permute-start | bytes 3145736 | tf_op jit(solution)/shard_map/ppermute | solution.py:547
  81.4 1.7 %add.154 = f32[2,256,512]{2,1,0:T(8,128)S(1)} add(f32[2,256,512]{2,1,0:T(8,128)} %get-tuple-element.28, f32[2,256,512]{2,1,0:T(8,128)} %collective-permute-done.10) | non-fusion elementwise | flops 262144 | bytes 3145728 | tf_op jit(solution)/shard_map/add | solution.py:547
  84.3 1.5 collective-permute-start.11
  87.0 5.3 %collective-permute-start.5 = (f32[1,256,512]{2,1,0:T(8,128)}, f32[1,256,512]{2,1,0:T(8,128)}, u32[]{:S(2)}, u32[]{:S(2)}) collective-permute-start(f32[1,256,512]{2,1,0:T(8,128)} %get-tuple-element.24), channel_id=1, source_target_pairs={{0,8},{8,0},{16,24},{24,16},{1,9},{9,1},{17,25},{25,17},{2,10},{10... | collective-permute-start | bytes 1572872 | tf_op jit(solution)/shard_map/ppermute | solution.py:537
  92.3 11.6 %collective-permute-done.6 = f32[2,256,512]{2,1,0:T(8,128)S(1)} collective-permute-done((f32[2,256,512]{2,1,0:T(8,128)}, f32[2,256,512]{2,1,0:T(8,128)S(1)}, u32[]{:S(2)}, u32[]{:S(2)}) %collective-permute-start.6) | collective-permute-done | bytes 1048608 | tf_op jit(solution)/shard_map/ppermute | solution.py:547
  106.0 9.1 %collective-permute-done.9 = f32[1,256,512]{2,1,0:T(8,128)} collective-permute-done((f32[1,256,512]{2,1,0:T(8,128)}, f32[1,256,512]{2,1,0:T(8,128)}, u32[]{:S(2)}, u32[]{:S(2)}) %collective-permute-start.9) | collective-permute-done | bytes 524320 | tf_op jit(solution)/shard_map/ppermute | solution.py:537
  116.5 2.4 %add_add_fusion = f32[1,256,512]{2,1,0:T(8,128)} fusion(f32[1,256,512]{2,1,0:T(8,128)} %collective-permute-done.11, f32[1,256,512]{2,1,0:T(8,128)} %collective-permute-done.12, f32[1,256,512]{2,1,0:T(8,128)S(1)} %copy-done.3, f32[1,256,512]{2,1,0:T(8,128)} %collective-permute-done.9), kind=kLoop, calls=%fused_computation | loop fusion | flops 393216 | bytes 2621440 | tf_op jit(solution)/shard_map/add | solution.py:541
  118.9 3.5 %all-to-all-start.1 = ((f32[8,32,512]{2,1,0:T(8,128)}), f32[8,32,512]{2,1,0:T(8,128)S(1)}, u32[]{:S(2)}, u32[]{:S(2)}) async-start(f32[8,32,512]{2,1,0:T(8,128)} %bitcast.7), calls=%async_computation.1 | async-start | bytes 1048576 | tf_op jit(solution)/shard_map/all_to_all | solution.py:521
  122.4 2.5 %collective-permute-done.5 = f32[1,256,512]{2,1,0:T(8,128)} collective-permute-done((f32[1,256,512]{2,1,0:T(8,128)}, f32[1,256,512]{2,1,0:T(8,128)}, u32[]{:S(2)}, u32[]{:S(2)}) %collective-permute-start.5) | collective-permute-done | bytes 524320 | tf_op jit(solution)/shard_map/ppermute | solution.py:537
  124.9 6.9 %collective-permute-done.8 = f32[1,256,512]{2,1,0:T(8,128)} collective-permute-done((f32[1,256,512]{2,1,0:T(8,128)}, f32[1,256,512]{2,1,0:T(8,128)}, u32[]{:S(2)}, u32[]{:S(2)}) %collective-permute-start.8) | collective-permute-done | bytes 524320 | tf_op jit(solution)/shard_map/ppermute | solution.py:536
  131.7 2.2 %add_add_fusion.1 = f32[1,256,512]{2,1,0:T(8,128)} fusion(f32[1,256,512]{2,1,0:T(8,128)S(1)} %collective-permute-done.7, f32[1,256,512]{2,1,0:T(8,128)} %collective-permute-done.8, f32[1,256,512]{2,1,0:T(8,128)S(1)} %copy-done.2, f32[1,256,512]{2,1,0:T(8,128)} %collective-permute-done.5), kind=kLoop, calls=%fused_computation.2 | loop fusion | flops 393216 | bytes 2621440 | tf_op jit(solution)/shard_map/add | solution.py:541
  134.0 3.5 %all-to-all-start = ((f32[8,32,512]{2,1,0:T(8,128)}), f32[8,32,512]{2,1,0:T(8,128)S(1)}, u32[]{:S(2)}, u32[]{:S(2)}) async-start(f32[8,32,512]{2,1,0:T(8,128)} %bitcast.6), calls=%async_computation | async-start | bytes 1048576 | tf_op jit(solution)/shard_map/all_to_all | solution.py:521
  137.8 1.4 shard_map.95.refs_0_
  139.3 7.9 %all-to-all-done.received = f32[8,32,512]{2,1,0:T(8,128)S(1)} async-done(((f32[8,32,512]{2,1,0:T(8,128)}), f32[8,32,512]{2,1,0:T(8,128)S(1)}, u32[]{:S(2)}, u32[]{:S(2)}) %all-to-all-start) | async-done | bytes 524320 | tf_op jit(solution)/shard_map/all_to_all | solution.py:521
  147.2 1.4 shard_map.96
  (48 shorter events, 15.3 us)
Async XLA Ops:
  5.0 31.0 %collective-permute-start.3 = (f32[7,96,256]{2,1,0:T(8,128)}, f32[7,96,256]{2,1,0:T(8,128)S(1)}, u32[]{:S(2)}, u32[]{:S(2)}) collective-permute-start(f32[7,96,256]{2,1,0:T(8,128)} %get-tuple-element.18.later), channel_id=1, source_target_pairs={{0,1},{1,2},{2,3},{3,4},{4,5},{5,6},{6,7},{8,9},{9,10},{10,11},{11... | collective-permute-start | bytes 2064392 | tf_op jit(solution)/shard_map/ppermute | solution.py:486
  7.4 17.9 %copy-start.4 = (f32[4]{0:T(128)S(1)}, f32[4]{0:T(128)}, u32[]{:S(2)}) copy-start(f32[4]{0:T(128)} %param.12) | copy-start | bytes 52
  7.4 28.6 %collective-permute-start.4 = (f32[7,96,256]{2,1,0:T(8,128)}, f32[7,96,256]{2,1,0:T(8,128)}, u32[]{:S(2)}, u32[]{:S(2)}) collective-permute-start(f32[7,96,256]{2,1,0:T(8,128)} %get-tuple-element.17.earlier), channel_id=1, source_target_pairs={{1,0},{2,1},{3,2},{4,3},{5,4},{6,5},{7,6},{9,8},{10,9},{11,10},{12... | collective-permute-start | bytes 2064392 | tf_op jit(solution)/shard_map/ppermute | solution.py:486
  22.1 4.2 %collective-permute-start = (f32[12,128]{1,0:T(8,128)}, f32[12,128]{1,0:T(8,128)S(1)}, u32[]{:S(2)}, u32[]{:S(2)}) collective-permute-start(f32[12,128]{1,0:T(8,128)} %get-tuple-element.19), channel_id=1, source_target_pairs={{0,1},{1,0},{2,3},{3,2},{4,5},{5,4},{6,7},{7,6},{8,9},{9,8},{10,11... | collective-permute-start | bytes 18440 | tf_op jit(solution)/shard_map/ppermute | solution.py:467
  27.0 3.7 %collective-permute-start.1 = (f32[12,128]{1,0:T(8,128)S(1)}, f32[12,128]{1,0:T(8,128)S(1)}, u32[]{:S(2)}, u32[]{:S(2)}) collective-permute-start(f32[12,128]{1,0:T(8,128)S(1)} %add.126), channel_id=1, source_target_pairs={{0,2},{1,3},{2,0},{3,1},{4,6},{5,7},{6,4},{7,5},{8,10},{9,11},{10,... | collective-permute-start | bytes 18440 | tf_op jit(solution)/shard_map/ppermute | solution.py:467
  30.7 4.5 %collective-permute-start.2 = (f32[12,128]{1,0:T(8,128)S(1)}, f32[12,128]{1,0:T(8,128)S(1)}, u32[]{:S(2)}, u32[]{:S(2)}) collective-permute-start(f32[12,128]{1,0:T(8,128)S(1)} %add.127), channel_id=1, source_target_pairs={{0,4},{1,5},{2,6},{3,7},{4,0},{5,1},{6,2},{7,3},{8,12},{9,13},{10,... | collective-permute-start | bytes 18440 | tf_op jit(solution)/shard_map/ppermute | solution.py:467
  36.0 0.9 copy-start.5
  55.5 25.9 %collective-permute-start.10 = (f32[2,256,512]{2,1,0:T(8,128)}, f32[2,256,512]{2,1,0:T(8,128)}, u32[]{:S(2)}, u32[]{:S(2)}) collective-permute-start(f32[2,256,512]{2,1,0:T(8,128)} %get-tuple-element.28), channel_id=1, source_target_pairs={{0,8},{24,16},{1,9},{25,17},{2,10},{26,18},{3,11},{27,19},{4,12},{... | collective-permute-start | bytes 3145736 | tf_op jit(solution)/shard_map/ppermute | solution.py:547
  78.6 25.4 %copy-start.1 = (f32[2,256,512]{2,1,0:T(8,128)S(1)}, f32[2,256,512]{2,1,0:T(8,128)}, u32[]{:S(2)}) copy-start(f32[2,256,512]{2,1,0:T(8,128)} %get-tuple-element.25) | copy-start | bytes 3145732
  78.6 25.3 %collective-permute-start.6 = (f32[2,256,512]{2,1,0:T(8,128)}, f32[2,256,512]{2,1,0:T(8,128)S(1)}, u32[]{:S(2)}, u32[]{:S(2)}) collective-permute-start(f32[2,256,512]{2,1,0:T(8,128)} %get-tuple-element.25), channel_id=1, source_target_pairs={{0,8},{24,16},{1,9},{25,17},{2,10},{26,18},{3,11},{27,19},{4,12},{... | collective-permute-start | bytes 3145736 | tf_op jit(solution)/shard_map/ppermute | solution.py:547
  80.2 34.9 %collective-permute-start.9 = (f32[1,256,512]{2,1,0:T(8,128)}, f32[1,256,512]{2,1,0:T(8,128)}, u32[]{:S(2)}, u32[]{:S(2)}) collective-permute-start(f32[1,256,512]{2,1,0:T(8,128)} %get-tuple-element.27), channel_id=1, source_target_pairs={{0,8},{8,0},{16,24},{24,16},{1,9},{9,1},{17,25},{25,17},{2,10},{10... | collective-permute-start | bytes 1572872 | tf_op jit(solution)/shard_map/ppermute | solution.py:537
  83.2 33.3 %copy-start.3 = (f32[1,256,512]{2,1,0:T(8,128)S(1)}, f32[1,256,512]{2,1,0:T(8,128)}, u32[]{:S(2)}) copy-start(f32[1,256,512]{2,1,0:T(8,128)} %get-tuple-element.26) | copy-start | bytes 1572868
  84.3 32.2 %collective-permute-start.11 = (f32[1,256,512]{2,1,0:T(8,128)}, f32[1,256,512]{2,1,0:T(8,128)}, u32[]{:S(2)}, u32[]{:S(2)}) collective-permute-start(f32[1,256,512]{2,1,0:T(8,128)} %get-tuple-element.30), channel_id=1, source_target_pairs={{8,16},{16,8},{9,17},{17,9},{10,18},{18,10},{11,19},{19,11},{12,20... | collective-permute-start | bytes 1572872 | tf_op jit(solution)/shard_map/ppermute | solution.py:535
  85.7 30.7 %collective-permute-start.12 = (f32[1,256,512]{2,1,0:T(8,128)}, f32[1,256,512]{2,1,0:T(8,128)}, u32[]{:S(2)}, u32[]{:S(2)}) collective-permute-start(f32[1,256,512]{2,1,0:T(8,128)} %get-tuple-element.29), channel_id=1, source_target_pairs={{8,24},{16,0},{9,25},{17,1},{10,26},{18,2},{11,27},{19,3},{12,28},... | collective-permute-start | bytes 1572872 | tf_op jit(solution)/shard_map/ppermute | solution.py:536
  87.0 44.7 %copy-start.2 = (f32[1,256,512]{2,1,0:T(8,128)S(1)}, f32[1,256,512]{2,1,0:T(8,128)}, u32[]{:S(2)}) copy-start(f32[1,256,512]{2,1,0:T(8,128)} %get-tuple-element.23) | copy-start | bytes 1572868
  87.0 37.8 %collective-permute-start.5 = (f32[1,256,512]{2,1,0:T(8,128)}, f32[1,256,512]{2,1,0:T(8,128)}, u32[]{:S(2)}, u32[]{:S(2)}) collective-permute-start(f32[1,256,512]{2,1,0:T(8,128)} %get-tuple-element.24), channel_id=1, source_target_pairs={{0,8},{8,0},{16,24},{24,16},{1,9},{9,1},{17,25},{25,17},{2,10},{10... | collective-permute-start | bytes 1572872 | tf_op jit(solution)/shard_map/ppermute | solution.py:537
  105.2 32.6 %copy-start = (bf16[2,512,512]{2,1,0:T(8,128)(2,1)S(1)}, bf16[2,512,512]{2,1,0:T(8,128)(2,1)}, u32[]{:S(2)}) copy-start(bf16[2,512,512]{2,1,0:T(8,128)(2,1)} %constant.65.clone.table) | copy-start | bytes 3145732
  105.2 19.7 %collective-permute-start.7 = (f32[1,256,512]{2,1,0:T(8,128)}, f32[1,256,512]{2,1,0:T(8,128)S(1)}, u32[]{:S(2)}, u32[]{:S(2)}) collective-permute-start(f32[1,256,512]{2,1,0:T(8,128)} %get-tuple-element.32), channel_id=1, source_target_pairs={{8,16},{16,8},{9,17},{17,9},{10,18},{18,10},{11,19},{19,11},{12,20... | collective-permute-start | bytes 1572872 | tf_op jit(solution)/shard_map/ppermute | solution.py:535
  115.1 16.6 %collective-permute-start.8 = (f32[1,256,512]{2,1,0:T(8,128)}, f32[1,256,512]{2,1,0:T(8,128)}, u32[]{:S(2)}, u32[]{:S(2)}) collective-permute-start(f32[1,256,512]{2,1,0:T(8,128)} %get-tuple-element.31), channel_id=1, source_target_pairs={{8,24},{16,0},{9,25},{17,1},{10,26},{18,2},{11,27},{19,3},{12,28},... | collective-permute-start | bytes 1572872 | tf_op jit(solution)/shard_map/ppermute | solution.py:536
  118.9 15.1 %all-to-all-start.1 = ((f32[8,32,512]{2,1,0:T(8,128)}), f32[8,32,512]{2,1,0:T(8,128)S(1)}, u32[]{:S(2)}, u32[]{:S(2)}) async-start(f32[8,32,512]{2,1,0:T(8,128)} %bitcast.7), calls=%async_computation.1 | async-start | bytes 1048576 | tf_op jit(solution)/shard_map/all_to_all | solution.py:521
  134.0 13.2 %all-to-all-start = ((f32[8,32,512]{2,1,0:T(8,128)}), f32[8,32,512]{2,1,0:T(8,128)S(1)}, u32[]{:S(2)}, u32[]{:S(2)}) async-start(f32[8,32,512]{2,1,0:T(8,128)} %bitcast.6), calls=%async_computation | async-start | bytes 1048576 | tf_op jit(solution)/shard_map/all_to_all | solution.py:521
